TPU v7x, 512 devices: a whole 4x4x16 slice. The times are simulated.
512 devices in a mesh: obs: 64 (over z, x), mem: 8 (over y, core).
Axes of the slice: x: 4, y: 4, z: 16, core: 2. Of those that a mesh axis runs over, the one named last changes fastest.
Arguments:
- anomalies: bfloat16 [256, 131072], P('mem', 'obs'), may hold values from -4 to 4
- innovations: float32 [256, 131072], P('mem', 'obs'), may hold values from -108 to 108
- obs_error: float32 [131072], P('obs'), may hold values from 1 to 4
- positions: bfloat16 [2, 131072], P(None, 'obs'), may hold values from 0 to 16, as said below
- pair_far: int32 [256], P('obs'), may hold values from 0 to 1, as said below
Outputs:
- solution: float32 [256, 131072], P('mem', 'obs')
- residual: float32 [256, 131072], P('mem', 'obs')
Inputs may be any that keep to these rules, and one draw needn't show every extreme that they name: pair_far[a] is 1 when the block pair (a, a + 2) is listed and 0 otherwise; it is 0 for the last two blocks. positions[0, n] lies in [0, 1]; positions[1, n] lies in [0, 16].
All inputs are finite; a program needn't handle non-finite values.
Results may differ from a plain program's by a relative error of at most 0.0003.
Values may be sent and summed in bfloat16 or wider, within the bound.
A program may use at most 64 MiB of HBM per device.

v0:
```python
import jax
import jax.numpy as jnp
from jax import lax
from jax.sharding import PartitionSpec as P

B = 512
ITERS = 2


epsilon = 1e-06
precise = lax.Precision.HIGHEST


def shifted(block, axis, distance):
    devices = range(lax.axis_size(axis))
    route = [(i - distance, i) for i in devices if i - distance in devices]
    return lax.ppermute(block, axis, route)


def gaspari(distance):
    inner_part = (
        ((-0.25 * distance + 0.5) * distance + 0.625) * distance - 5.0 / 3.0
    ) * distance * distance + 1.0
    outer_arg = jnp.maximum(distance, 1.0)
    outer_part = (
        ((((distance / 12.0 - 0.5) * distance + 0.625) * distance + 5.0 / 3.0) * distance - 5.0)
        * distance
        + 4.0
        - 2.0 / (3.0 * outer_arg)
    )
    return jnp.where(distance <= 1.0, inner_part, jnp.where(distance < 2.0, outer_part, 0.0))


def pair_taper(first_places, second_places, offset):
    first_places = first_places.astype(jnp.float32)
    second_places = second_places.astype(jnp.float32)
    along_gap = first_places[..., 0, :, None] - second_places[..., 0, None, :] - offset
    across = first_places[..., 1, :, None] - second_places[..., 1, None, :]
    return gaspari(jnp.sqrt(along_gap * along_gap + across * across))


def add_into(totals, values, location):
    current = lax.dynamic_slice_in_dim(totals, location, values.shape[1], 1)
    return lax.dynamic_update_slice_in_dim(totals, current + values, location, 1)


def keep_same(values):
    return values


def body(anomalies, innovations, obs_error, positions, pair_far):
    block_size = B
    half_width = B // 2
    blocks_here = pair_far.shape[0]
    local_width = blocks_here * block_size
    members = anomalies.shape[0] * lax.axis_size("mem")
    inverse_count = 1.0 / (members - 1)
    ensemble = lax.all_gather(anomalies, "mem", axis=0, tiled=True)
    ensemble_after, places_after = shifted((ensemble, positions), "obs", -1)
    places_frame = jnp.concatenate([positions, places_after], axis=1)

    def spatial_total(values):
        return lax.psum(jnp.sum(values, axis=1), "obs")

    solution = jnp.zeros_like(innovations)
    residual = innovations
    direction = innovations
    norm_now = spatial_total(residual * residual)
    for step_index in range(ITERS):
        vector_after = shifted(direction, "obs", -1)
        vector_frame = jnp.concatenate([direction, vector_after], axis=1)

        def visit_block(slot_index, totals):
            first_start = slot_index * block_size
            first_ens = lax.dynamic_slice_in_dim(ensemble, first_start, block_size, 1)
            first_vec = lax.dynamic_slice_in_dim(vector_frame, first_start, block_size, 1)
            first_places = lax.dynamic_slice_in_dim(places_frame, first_start, block_size, 1)
            for offset in (0, 1, 2):

                def pair_product(totals, offset=offset):
                    partner = slot_index + offset
                    from_here = lax.dynamic_slice_in_dim(
                        ensemble, jnp.minimum(partner, blocks_here - 1) * block_size, block_size, 1
                    )
                    from_after = lax.dynamic_slice_in_dim(
                        ensemble_after,
                        jnp.maximum(partner - blocks_here, 0) * block_size,
                        block_size,
                        1,
                    )
                    partner_ens = jnp.where(partner < blocks_here, from_here, from_after)
                    for half_index in range(2):
                        column = partner * block_size + half_index * half_width
                        half_ens = partner_ens[
                            :, half_index * half_width : (half_index + 1) * half_width
                        ]
                        half_places = lax.dynamic_slice_in_dim(places_frame, column, half_width, 1)
                        half_vec = lax.dynamic_slice_in_dim(vector_frame, column, half_width, 1)
                        raw_product = lax.dot_general(
                            first_ens,
                            half_ens,
                            (((0,), (0,)), ((), ())),
                            preferred_element_type=jnp.float32,
                        )
                        coupling = (
                            raw_product
                            * inverse_count
                            * pair_taper(first_places, half_places, float(offset))
                        )
                        into_first = lax.dot_general(
                            half_vec,
                            coupling,
                            (((1,), (1,)), ((), ())),
                            precision=precise,
                            preferred_element_type=jnp.float32,
                        )
                        totals = add_into(totals, into_first, first_start)
                        if offset > 0:
                            into_partner = jnp.dot(
                                first_vec,
                                coupling,
                                precision=precise,
                                preferred_element_type=jnp.float32,
                            )
                            totals = add_into(totals, into_partner, column)
                    return totals

                if offset == 2:
                    totals = lax.cond(pair_far[slot_index] == 1, pair_product, keep_same, totals)
                else:
                    totals = pair_product(totals)
            return totals

        initial = jnp.zeros((direction.shape[0], 2 * local_width), jnp.float32)
        totals = lax.fori_loop(0, blocks_here, visit_block, initial)
        returned = shifted(totals[:, local_width:], "obs", 1)
        operated = totals[:, :local_width] + returned + obs_error[None, :] * direction
        step_size = norm_now / spatial_total(direction * operated)
        solution = solution + step_size[:, None] * direction
        residual = residual - step_size[:, None] * operated
        if step_index + 1 < ITERS:
            norm_next = spatial_total(residual * residual)
            direction = residual + (norm_next / (norm_now + epsilon))[:, None] * direction
            norm_now = norm_next
    return (solution, residual)


def solution(mesh):
    in_specs = (P("mem", "obs"), P("mem", "obs"), P("obs"), P(None, "obs"), P("obs"))
    out_specs = (P("mem", "obs"), P("mem", "obs"))
    return jax.shard_map(body, mesh=mesh, in_specs=in_specs, out_specs=out_specs, check_vma=False)
```

profile of v0, /device:TPU:128, one launch (start us, length us, event | category | flops | bytes accessed | tf_op | source)
XLA Modules:
  0.0 690.8 jit_solution(5775112893785921618)
XLA Ops:
  7.9 36.4 %all-gather.2.cloned.1.call-done = bf16[256,2048]{1,0:T(8,128)(2,1)} async-done(((bf16[32,2048]{1,0:T(8,128)(2,1)}), bf16[256,2048]{1,0:T(8,128)(2,1)}) %all-gather.2.cloned.1.call-update) | async-done | bytes 1048592 | tf_op jit(solution)/shard_map/all_gather | solution.py:58
  44.3 4.6 collective-permute-start.1
  48.9 2.8 collective-permute-start.2
  51.7 2.5 collective-permute-start
  54.2 18.6 %collective-permute-done.2 = bf16[2,2048]{1,0:T(2,128)(2,1)S(1)} collective-permute-done((bf16[2,2048]{1,0:T(2,128)(2,1)S(1)}, bf16[2,2048]{1,0:T(2,128)(2,1)S(1)}, u32[]{:S(2)}, u32[]{:S(2)}) %collective-permute-start.2) | collective-permute-done | bytes 8224 | tf_op jit(solution)/shard_map/ppermute | solution.py:17
  72.8 5.0 collective-permute-done
  77.8 1.8 pad_maximum_fusion
  80.3 51.3 %while.36 = (s32[]{:T(128)}, f32[32,4096]{1,0:T(8,128)S(1)}, s32[4]{0:T(128)S(1)}, f32[32,4096]{1,0:T(8,128)}, bf16[256,2048]{1,0:T(8,128)(2,1)S(1)}, /*index=5*...) while((s32[]{:T(128)}, f32[32,4096]{1,0:T(8,128)S(1)}, ...), condition=%wide.region_5.6_spmd, body=%wide.region_2.5_spmd.sunk | while | flops 933628928 | bytes 17731748 | solution.py:135
  82.1 1.3 fusion.288
  84.3 1.4 fusion.290
  86.7 1.3 fusion.293
  89.2 0.9 fusion.295
  90.1 1.3 fusion.296
  94.9 1.3 fusion.288
  97.2 1.4 fusion.290
  98.6 0.9 fusion.292
  99.5 1.3 fusion.293
  102.0 0.9 fusion.295
  103.0 1.3 fusion.296
  107.8 1.3 fusion.288
  110.0 1.4 fusion.290
  112.3 1.3 fusion.293
  114.9 0.9 fusion.295
  115.8 1.3 fusion.296
  120.6 1.3 fusion.288
  122.9 1.4 fusion.290
  125.2 1.3 fusion.293
  127.7 0.9 fusion.295
  128.6 1.3 fusion.296
  131.7 20.8 %collective-permute-start.3 = (f32[32,2048]{1,0:T(8,128)S(1)}, f32[32,2048]{1,0:T(8,128)S(1)}, u32[]{:S(2)}, u32[]{:S(2)}) collective-permute-start(f32[32,2048]{1,0:T(8,128)S(1)} %slice.469), channel_id=1, source_target_pairs={{0,8},{8,16},{16,24},{24,32},{32,40},{40,48},{48,56},{56,64},{64,7... | collective-permute-start | bytes 786440 | tf_op jit(solution)/shard_map/ppermute | solution.py:17
  152.5 16.2 %collective-permute-done.3 = f32[32,2048]{1,0:T(8,128)S(1)} collective-permute-done((f32[32,2048]{1,0:T(8,128)S(1)}, f32[32,2048]{1,0:T(8,128)S(1)}, u32[]{:S(2)}, u32[]{:S(2)}) %collective-permute-start.3) | collective-permute-done | bytes 262176 | tf_op jit(solution)/shard_map/ppermute | solution.py:17
  168.9 139.7 %all-reduce = (f32[32]{0:T(128)S(1)}, f32[32]{0:T(128)S(1)}) all-reduce(f32[32]{0:T(128)S(1)} %get-tuple-element.663, f32[32]{0:T(128)S(1)} %get-tuple-element.662), channel_id=1, replica_groups=mesh['obs'=64,'mem'=8] {'obs'}, use_global_device_ids=true, to_apply=%region_1.0 | all-reduce | flops 64 | bytes 512 | tf_op jit(solution)/shard_map/psum | solution.py:63
  308.8 138.4 %psum.30 = f32[32]{0:T(128)S(1)} all-reduce(f32[32]{0:T(128)S(1)} %get-tuple-element.694), channel_id=1, replica_groups=mesh['obs'=64,'mem'=8] {'obs'}, use_global_device_ids=true, to_apply=%region_9.10 | all-reduce | flops 32 | bytes 256 | tf_op jit(solution)/shard_map/psum | solution.py:63
  447.4 3.7 collective-permute-start.4
  451.1 4.5 collective-permute-done.4
  456.5 51.5 %while.37 = (s32[]{:T(128)}, f32[32,4096]{1,0:T(8,128)S(1)}, s32[4]{0:T(128)S(1)}, f32[32,4096]{1,0:T(8,128)}, bf16[256,2048]{1,0:T(8,128)(2,1)S(1)}, /*index=5*...) while((s32[]{:T(128)}, f32[32,4096]{1,0:T(8,128)S(1)}, ...), condition=%wide.region_13.14_spmd, body=%wide.region_10.13_spmd.sunk | while | flops 933628928 | bytes 17731748 | solution.py:135
  458.4 1.3 fusion.322
  460.7 1.4 fusion.324
  462.1 0.9 fusion.326
  463.0 1.3 fusion.327
  465.5 0.9 fusion.329
  466.4 1.3 fusion.330
  471.3 1.3 fusion.322
  473.5 1.4 fusion.324
  474.9 0.9 fusion.326
  475.8 1.3 fusion.327
  478.4 0.9 fusion.329
  479.3 1.3 fusion.330
  484.2 1.3 fusion.322
  486.4 1.4 fusion.324
  487.8 0.9 fusion.326
  488.7 1.3 fusion.327
  491.3 0.9 fusion.329
  492.2 1.3 fusion.330
  497.0 1.3 fusion.322
  499.3 1.4 fusion.324
  500.7 0.9 fusion.326
  501.6 1.3 fusion.327
  504.1 0.9 fusion.329
  505.1 1.3 fusion.330
  508.1 21.2 %collective-permute-start.5 = (f32[32,2048]{1,0:T(8,128)S(1)}, f32[32,2048]{1,0:T(8,128)S(1)}, u32[]{:S(2)}, u32[]{:S(2)}) collective-permute-start(f32[32,2048]{1,0:T(8,128)S(1)} %slice.471), channel_id=1, source_target_pairs={{0,8},{8,16},{16,24},{24,32},{32,40},{40,48},{48,56},{56,64},{64,7... | collective-permute-start | bytes 786440 | tf_op jit(solution)/shard_map/ppermute | solution.py:17
  529.3 13.6 %collective-permute-done.5 = f32[32,2048]{1,0:T(8,128)S(1)} collective-permute-done((f32[32,2048]{1,0:T(8,128)S(1)}, f32[32,2048]{1,0:T(8,128)S(1)}, u32[]{:S(2)}, u32[]{:S(2)}) %collective-permute-start.5) | collective-permute-done | bytes 262176 | tf_op jit(solution)/shard_map/ppermute | solution.py:17
  543.0 140.0 %psum.31 = f32[32]{0:T(128)S(1)} all-reduce(f32[32]{0:T(128)S(1)} %multiply_reduce_fusion), channel_id=1, replica_groups=mesh['obs'=64,'mem'=8] {'obs'}, use_global_device_ids=true, to_apply=%region_15.16 | all-reduce | flops 32 | bytes 256 | tf_op jit(solution)/shard_map/psum | solution.py:63
  683.1 0.9 multiply_subtract_fusion
  (160 shorter events, 44.4 us)
Async XLA Ops:
  7.2 41.7 %copy-start.14 = (bf16[2,2048]{1,0:T(2,128)(2,1)S(1)}, bf16[2,2048]{1,0:T(2,128)(2,1)}, u32[]{:S(2)}) copy-start(bf16[2,2048]{1,0:T(2,128)(2,1)} %param.16) | copy-start | bytes 24580
  7.2 37.1 %all-gather.2.cloned.1.call-start = ((), (), s32[]{:S(2)}) async-start(), calls=%async_computation | async-start | bytes 1179648 | tf_op jit(solution)/shard_map/all_gather | solution.py:58
  44.3 35.4 %copy-start = (bf16[256,2048]{1,0:T(8,128)(2,1)S(1)}, bf16[256,2048]{1,0:T(8,128)(2,1)}, u32[]{:S(2)}) copy-start(bf16[256,2048]{1,0:T(8,128)(2,1)} %all-gather.2.cloned.1.call-done) | copy-start | bytes 3145732
  44.3 35.4 %collective-permute-start.1 = (bf16[256,2048]{1,0:T(8,128)(2,1)}, bf16[256,2048]{1,0:T(8,128)(2,1)S(1)}, u32[]{:S(2)}, u32[]{:S(2)}) collective-permute-start(bf16[256,2048]{1,0:T(8,128)(2,1)} %all-gather.2.cloned.1.call-done), channel_id=1, source_target_pairs={{8,0},{16,8},{24,16},{32,24},{40,32},{48,40},{56,48},{64,56},{72,6... | collective-permute-start | bytes 3145736 | tf_op jit(solution)/shard_map/ppermute | solution.py:17
  48.9 23.9 %collective-permute-start.2 = (bf16[2,2048]{1,0:T(2,128)(2,1)S(1)}, bf16[2,2048]{1,0:T(2,128)(2,1)S(1)}, u32[]{:S(2)}, u32[]{:S(2)}) collective-permute-start(bf16[2,2048]{1,0:T(2,128)(2,1)S(1)} %copy-done.14), channel_id=1, source_target_pairs={{8,0},{16,8},{24,16},{32,24},{40,32},{48,40},{56,48},{64,56},{72,6... | collective-permute-start | bytes 24584 | tf_op jit(solution)/shard_map/ppermute | solution.py:17
  51.7 26.2 %collective-permute-start = (f32[32,2048]{1,0:T(8,128)}, f32[32,2048]{1,0:T(8,128)S(1)}, u32[]{:S(2)}, u32[]{:S(2)}) collective-permute-start(f32[32,2048]{1,0:T(8,128)} %param.14), channel_id=1, source_target_pairs={{8,0},{16,8},{24,16},{32,24},{40,32},{48,40},{56,48},{64,56},{72,6... | collective-permute-start | bytes 786440 | tf_op jit(solution)/shard_map/ppermute | solution.py:17
  79.6 0.7 copy-start.15
  84.3 1.4 copy-start.1
  97.2 1.4 copy-start.1
  110.0 1.4 copy-start.1
  122.9 1.4 copy-start.1
  131.6 37.1 %copy-start.3 = (f32[32,2048]{1,0:T(8,128)S(1)}, f32[32,2048]{1,0:T(8,128)}, u32[]{:S(2)}) copy-start(f32[32,2048]{1,0:T(8,128)} %param.14) | copy-start | bytes 786436
  131.6 37.1 %copy-start.13 = (f32[2048]{0:T(1024)S(1)}, f32[2048]{0:T(1024)}, u32[]{:S(2)}) copy-start(f32[2048]{0:T(1024)} %param.15) | copy-start | bytes 24580
  131.7 37.1 %collective-permute-start.3 = (f32[32,2048]{1,0:T(8,128)S(1)}, f32[32,2048]{1,0:T(8,128)S(1)}, u32[]{:S(2)}, u32[]{:S(2)}) collective-permute-start(f32[32,2048]{1,0:T(8,128)S(1)} %slice.469), channel_id=1, source_target_pairs={{0,8},{8,16},{16,24},{24,32},{32,40},{40,48},{48,56},{56,64},{64,7... | collective-permute-start | bytes 786440 | tf_op jit(solution)/shard_map/ppermute | solution.py:17
  308.8 138.5 %copy-start.11 = (f32[32,2048]{1,0:T(8,128)}, f32[32,2048]{1,0:T(8,128)S(1)}, u32[]{:S(2)}) copy-start(f32[32,2048]{1,0:T(8,128)S(1)} %get-tuple-element.695) | copy-start | bytes 786436
  447.4 9.1 %copy-start.9 = (f32[32,2048]{1,0:T(8,128)}, f32[32,2048]{1,0:T(8,128)S(1)}, u32[]{:S(2)}) copy-start(f32[32,2048]{1,0:T(8,128)S(1)} %multiply_add_fusion.2) | copy-start | bytes 786436
  447.4 8.3 %collective-permute-start.4 = (f32[32,2048]{1,0:T(8,128)S(1)}, f32[32,2048]{1,0:T(8,128)S(1)}, u32[]{:S(2)}, u32[]{:S(2)}) collective-permute-start(f32[32,2048]{1,0:T(8,128)S(1)} %multiply_add_fusion.2), channel_id=1, source_target_pairs={{8,0},{16,8},{24,16},{32,24},{40,32},{48,40},{56,48},{64,56},{72,6... | collective-permute-start | bytes 786440 | tf_op jit(solution)/shard_map/ppermute | solution.py:17
  460.6 1.4 copy-start.2
  473.5 1.4 copy-start.2
  486.4 1.4 copy-start.2
  499.3 1.4 copy-start.2
  508.1 34.8 %copy-start.10 = (f32[32,2048]{1,0:T(8,128)S(1)}, f32[32,2048]{1,0:T(8,128)}, u32[]{:S(2)}) copy-start(f32[32,2048]{1,0:T(8,128)} %copy-done.9) | copy-start | bytes 786436
  508.1 175.0 %copy-start.4 = (f32[32,2048]{1,0:T(8,128)S(1)}, f32[32,2048]{1,0:T(8,128)}, u32[]{:S(2)}) copy-start(f32[32,2048]{1,0:T(8,128)} %param.14) | copy-start | bytes 786436
  508.1 175.0 %copy-start.12 = (f32[32,2048]{1,0:T(8,128)S(1)}, f32[32,2048]{1,0:T(8,128)}, u32[]{:S(2)}) copy-start(f32[32,2048]{1,0:T(8,128)} %copy-done.11) | copy-start | bytes 786436
  508.1 34.8 %collective-permute-start.5 = (f32[32,2048]{1,0:T(8,128)S(1)}, f32[32,2048]{1,0:T(8,128)S(1)}, u32[]{:S(2)}, u32[]{:S(2)}) collective-permute-start(f32[32,2048]{1,0:T(8,128)S(1)} %slice.471), channel_id=1, source_target_pairs={{0,8},{8,16},{16,24},{24,32},{32,40},{40,48},{48,56},{56,64},{64,7... | collective-permute-start | bytes 786440 | tf_op jit(solution)/shard_map/ppermute | solution.py:17
Sparse Core Ops, SparseCore 0:
  10.2 34.0 all-gather.1
where the time goes:
time: 695 us; the launch traced here: 691 us
  blocking collectives  418 us (60%)
  waiting for transfers between devices  95 us (14%)
  matrix products  77.2 us (11%)
  starting transfers between devices  55.7 us (8%)
  between operations  14.2 us (2%)
  local copies, waits for them, and re-layouts  12.7 us (2%)
  other arithmetic  11 us (2%)
    psum x3, blocking collectives, spatial_total(): return lax.psum(jnp.sum(values, axis=1), 'obs')  418 us
    ppermute x6, waiting for transfers between devices, shifted(): return lax.ppermute(block, axis, route)  58 us
    ppermute x6, starting transfers between devices, shifted(): return lax.ppermute(block, axis, route)  55.6 us
    dot_general x32, matrix products, pair_product(): lax.dot_general(half_vec, coupling, (((1,), (1,)), ((), ())), precision=p...  42.8 us
    all_gather x1, waiting for transfers between devices, body(): ensemble = lax.all_gather(anomalies, 'mem', axis=0, tiled=True)  36.4 us
    dot_general x32, matrix products, pair_product(): lax.dot_general(first_ens, half_ens, (((0,), (0,)), ((), ())), preferred_...  28.8 us
  transfers between devices with their start and end apart: 7, of which 6 were waited for; matrix products, arithmetic and copies ran while one was open for 0% of the time, Pallas kernels for 0%

commit v1 on v0

v1 whole, which is shorter than its diff:
```python
import functools
import math

import jax
import jax.numpy as jnp
from jax import lax
from jax.experimental import pallas as pl
from jax.experimental.pallas import tpu as pltpu
from jax.sharding import PartitionSpec as P

B = 512
NX = 4
EPSILON = 1e-06
ROOT2 = math.sqrt(2.0)
SCALE = 48.0 * ROOT2
MESH = pl.DeviceIdType.MESH
CHUNK = 16
PAIRS = [(0, 2), (0, 3), (1, 2), (1, 3), (0, 1), (1, 4), (0, 0), (0, 4), (1, 1), (1, 5)]
NT = (((1,), (1,)), ((), ()))


def remote(src, dst, send, recv, device):
    return pltpu.make_async_remote_copy(
        src_ref=src, dst_ref=dst, send_sem=send, recv_sem=recv, device_id=device, device_id_type=MESH
    )


def kernel(
    block, nobs, nmem, nx,
    anom, innov, oerr, places, far, x_out, r_out,
    X, XT, U, V, UH, CH, CL, TP, RAW, PI, META, SC, PP, W, W2, W3, COEF, R1A, R2A, R1B, R2B,
    a_send, a_recv, f_send, f_recv, u_send, u_recv, m_send, m_recv, v_send, v_recv, w_send, w_recv,
    r1_send, r1_recv, r2_send, r2_recv, q1_send, q1_recv, q2_send, q2_recv,
):
    f32, bf16 = jnp.float32, jnp.bfloat16
    half = 2 * block
    rows = anom.shape[0]
    rows2 = 2 * rows
    nz = nobs // nx
    o = lax.axis_index("obs")
    mm = lax.axis_index("mem")
    c = lax.rem(mm, 2)
    y2 = mm - c
    pm = y2 + 1 - c
    z = lax.div(o, nx)
    x = lax.rem(o, nx)
    left = (lax.rem(o + nobs - 1 + c, nobs), pm)
    right = (lax.rem(o + c, nobs), pm)
    partner = (o, pm)
    far_to = (lax.rem(o + nobs + 1 - 2 * c, nobs), mm)
    far_from = (lax.rem(o + nobs - 1 + 2 * c, nobs), mm)
    off_chip = (lax.rem(o + nobs - 1 + 2 * c, nobs), pm)
    i1 = x * 2 + c

    def peer1(d):
        idx = lax.rem(i1 + d, 2 * nx)
        return (z * nx + lax.div(idx, 2), y2 + lax.rem(idx, 2))

    def peer2(d):
        return (lax.rem(z + d, nz) * nx + x, mm)

    barrier = pltpu.get_barrier_semaphore()
    peers = [(o, lax.rem(mm + d, nmem)) for d in range(1, nmem)]
    peers += [left, right, far_to, far_from]
    peers += [peer1(d) for d in range(1, 2 * nx)]
    peers += [peer2(d) for d in range(1, nz)]
    for peer in peers:
        pl.semaphore_signal(barrier, inc=1, device_id=peer, device_id_type=MESH)

    own_rows = pl.ds(pl.multiple_of(mm * rows, rows), rows)
    core_rows = pl.ds(pl.multiple_of(c * rows, rows), rows)
    partner_rows = pl.ds(pl.multiple_of((1 - c) * rows, rows), rows)
    own_half = pl.ds(pl.multiple_of(c * half, half), half)
    other_half = pl.ds(pl.multiple_of((1 - c) * half, half), half)
    pf = places[...].astype(f32) * ROOT2
    for h in range(2):
        flags = jnp.concatenate(
            [jnp.full((1, block), far[2 * h + b].astype(f32), f32) for b in range(2)], axis=1
        )
        META[1 - c + h] = jnp.concatenate(
            [pf[:, h * half : (h + 1) * half], flags, jnp.zeros((5, half), f32)], axis=0
        )
    X[1, own_rows, :] = anom[:, own_half]
    pl.semaphore_wait(barrier, len(peers))

    meta_copy = remote(META.at[1], META.at[2 - 2 * c], m_send, m_recv, off_chip)
    meta_copy.start()
    meta_back = remote(META.at[1], META.at[2 * c], m_send, m_recv, off_chip)

    a_out, a_in = [], []
    for d in range(1, nmem):
        to = lax.rem(mm + d, nmem)
        source = lax.rem(mm + nmem - d, nmem)
        to_half = pl.ds(pl.multiple_of(lax.rem(to, 2) * half, half), half)
        copy = remote(anom.at[:, to_half], X.at[1, own_rows, :], a_send.at[d], a_recv.at[d], (o, to))
        copy.start()
        a_out.append(copy)
        src_rows = pl.ds(pl.multiple_of(source * rows, rows), rows)
        a_in.append(remote(anom.at[:, own_half], X.at[1, src_rows, :], a_send.at[d], a_recv.at[d], (o, to)))

    def forward(d):
        source = lax.rem(mm + nmem - d, nmem)
        piece = pl.ds(pl.multiple_of(source * rows, rows), rows)
        if d > 0:
            a_in[d - 1].wait_recv()
        one = remote(X.at[1, piece, :], X.at[2, piece, :], f_send.at[0, d], f_recv.at[0, d], left)
        two = remote(X.at[1, piece, :], X.at[0, piece, :], f_send.at[1, d], f_recv.at[1, d], right)
        one.start()
        two.start()
        return [one, two]

    def forwarded(slot, d):
        source = lax.rem(pm + nmem - d, nmem)
        piece = pl.ds(pl.multiple_of(source * rows, rows), rows)
        way = 0 if slot == 2 else 1
        device = left if slot == 2 else right
        return remote(X.at[1, piece, :], X.at[slot, piece, :], f_send.at[way, d], f_recv.at[way, d], device)

    f_out = forward(0)

    u_out = [
        remote(innov.at[:, own_half], U.at[2, core_rows, :], u_send.at[0], u_recv.at[0], left),
        remote(innov.at[:, own_half], U.at[0, core_rows, :], u_send.at[1], u_recv.at[1], right),
        remote(innov.at[:, other_half], U.at[1, core_rows, :], u_send.at[2], u_recv.at[2], partner),
        remote(innov.at[:, other_half], U.at[2 * c, core_rows, :], u_send.at[3], u_recv.at[3], far_to),
    ]
    u_in = [
        remote(innov.at[:, own_half], U.at[2, partner_rows, :], u_send.at[0], u_recv.at[0], left),
        remote(innov.at[:, own_half], U.at[0, partner_rows, :], u_send.at[1], u_recv.at[1], right),
        remote(innov.at[:, other_half], U.at[1, partner_rows, :], u_send.at[2], u_recv.at[2], partner),
        remote(innov.at[:, other_half], U.at[2 * c, core_rows, :], u_send.at[3], u_recv.at[3], far_to),
    ]
    for copy in u_out:
        copy.start()
    for h in range(2):
        U[1 - c + h, core_rows, :] = innov[:, h * half : (h + 1) * half]

    lanes = 128
    for k in range(half // lanes):
        for axis in range(2):
            line = META[1, axis : axis + 1, k * lanes : (k + 1) * lanes]
            PI[axis, k * lanes : (k + 1) * lanes, :] = jnp.broadcast_to(line, (lanes, lanes)).T

    def window(w):
        slot, part = divmod(w, 2)
        return slot, slice(part * block, (part + 1) * block)

    def taper(p):
        s, w = PAIRS[p]
        offset = w - 2 - s
        slot, cols = window(w)
        along = META[slot, 0:1, cols] + offset * ROOT2
        across = META[slot, 1:2, cols]
        near = abs(offset) < 2

        def step(k, carry):
            at = pl.multiple_of(k * CHUNK, CHUNK)
            mine = pl.ds(s * block + at, CHUNK)
            g = jnp.concatenate([PI[0, mine, :]] * (block // lanes), axis=1) - along
            h = jnp.concatenate([PI[1, mine, :]] * (block // lanes), axis=1) - across
            square = g * g + h * h
            if near:
                square = jnp.maximum(square, 1e-30)
            inverse = lax.rsqrt(square)
            y = square * inverse
            rest = jnp.maximum(2.0 * ROOT2 - y, 0.0)
            rest = rest * rest
            value = (rest * rest) * ((y - inverse) + 2.0 * ROOT2)
            if near:
                inner = (-3.0 * y + 0.125 * SCALE) * y + 0.3125 * SCALE / ROOT2
                inner = (inner * y - (5.0 / 6.0) * SCALE) * square + SCALE
                value = jnp.maximum(value, inner)
            TP[p, pl.ds(at, CHUNK), :] = value
            return carry

        lax.fori_loop(0, block // CHUNK, step, 0, unroll=2)

    for p in range(4):
        taper(p)
        if p == 0:
            f_out += forward(1)
        else:
            f_out += forward(2 * p) + forward(2 * p + 1) if 2 * p + 1 < nmem else []
    meta_back.wait_recv()
    for p in range(4, 10):
        taper(p)

    q = 2 * o + c
    first = jnp.where(q > 0, 1.0, 0.0).astype(f32)
    last = jnp.where(q < 2 * nobs - 1, 1.0, 0.0).astype(f32)
    factor = 1.0 / (SCALE * (rows * nmem - 1))
    for p, (s, w) in enumerate(PAIRS):
        offset = w - 2 - s
        line = jnp.full((1, block), factor, f32)
        if w < 2:
            line = line * first
        if w > 3:
            line = line * last
        if offset == 2:
            line = line * META[1, 2:3, s * block : (s + 1) * block]
        if offset == -2:
            line = line * META[0, 2:3, s * block : (s + 1) * block]
        SC[p : p + 1, :] = line

    for k in range(half // 256):
        XT[k * 256 : (k + 1) * 256, :] = X[1, :, k * 256 : (k + 1) * 256].T

    def couple(p):
        s, w = PAIRS[p]
        slot, cols = window(w)
        part = min(block, 256)
        for k in range(block // part):
            RAW[k * part : (k + 1) * part, :] = jnp.dot(
                XT[s * block + k * part : s * block + (k + 1) * part, :],
                X[slot, :, cols],
                preferred_element_type=f32,
            )

        def step(k, carry):
            at = pl.ds(pl.multiple_of(k * CHUNK, CHUNK), CHUNK)
            value = RAW[at, :] * TP[p, at, :]
            high = value.astype(bf16)
            CH[p, at, :] = high
            CL[p, at, :] = (value - high.astype(f32)).astype(bf16)
            return carry

        lax.fori_loop(0, block // CHUNK, step, 0, unroll=2)

    def split(values, w):
        high = values.astype(bf16)
        UH[w, 0:rows2, :] = high
        UH[w, rows2 : 2 * rows2, :] = (values - high.astype(f32)).astype(bf16)

    def product(p):
        s, w = PAIRS[p]
        full = lax.dot_general(UH[w], CH[p], NT, preferred_element_type=f32)
        low = lax.dot_general(UH[w, 0:rows2, :], CL[p], NT, preferred_element_type=f32)
        return (full[0:rows2] + full[rows2:] + low) * SC[p : p + 1, :]

    for copy in u_in:
        copy.wait_recv()
    for w in range(6):
        slot, cols = window(w)
        split(U[slot, :, cols], w)

    for s in range(2):
        cols = slice(s * block, (s + 1) * block)
        W[:, cols] = U[1, :, cols] * oerr[:, pl.ds(pl.multiple_of(c * half + s * block, block), block)]
    for p in range(10):
        if p == 4:
            for slot in (0, 2):
                for d in range(nmem):
                    forwarded(slot, d).wait_recv()
        couple(p)
        s = PAIRS[p][0]
        cols = slice(s * block, (s + 1) * block)
        W[:, cols] += product(p)
    V[1] = W[...]

    v_out = [
        remote(V.at[1], V.at[2], v_send.at[0], v_recv.at[0], left),
        remote(V.at[1], V.at[0], v_send.at[1], v_recv.at[1], right),
    ]
    for copy in v_out:
        copy.start()

    def lane_sums(value):
        total = value[:, 0:lanes]
        for k in range(1, half // lanes):
            total = total + value[:, k * lanes : (k + 1) * lanes]
        return total

    def total(count, one, two, one_sems, two_sems):
        row = jnp.sum(PP[0:count, :].T, axis=0, keepdims=True)
        out = []
        for buffer, index, size, peer, sems in (
            (one, i1, 2 * nx, peer1, one_sems),
            (two, z, nz, peer2, two_sems),
        ):
            buffer[pl.ds(index, 1), :] = row
            mine = buffer.at[pl.ds(index, 1), :]
            arrivals = []
            for d in range(1, size):
                copy = remote(mine, mine, sems[0].at[d], sems[1].at[d], peer(d))
                copy.start()
                out.append(copy)
                there = buffer.at[pl.ds(lax.rem(index + size - d, size), 1), :]
                arrivals.append(remote(mine, there, sems[0].at[d], sems[1].at[d], peer(d)))
            for copy in arrivals:
                copy.wait_recv()
            row = jnp.sum(buffer[...], axis=0, keepdims=True)
        return row, out

    def columns(lines):
        width = lines[0].shape[1]
        place = lax.broadcasted_iota(jnp.int32, (lanes, width), 0)
        table = jnp.broadcast_to(lines[0], (lanes, width))
        for k in range(1, len(lines)):
            table = jnp.where(place == k, lines[k], table)
        table = jnp.concatenate([table, jnp.zeros((lanes, lanes - width), f32)], axis=1)
        COEF[...] = table.T

    u0, u1 = U[1], V[1]
    PP[0:rows2, :] = lane_sums(u0 * u0)
    PP[rows2 : 2 * rows2, :] = lane_sums(u0 * u1)
    PP[2 * rows2 : 3 * rows2, :] = lane_sums(u1 * u1)
    PP[3 * rows2 : 4 * rows2, :] = jnp.zeros((rows2, lanes), f32)
    sums, s_out = total(4 * rows2, R1A, R2A, (r1_send, r1_recv), (r2_send, r2_recv))
    norm = sums[:, 0:rows2]
    size = norm / sums[:, rows2 : 2 * rows2]
    norm_next = size * size * sums[:, 2 * rows2 : 3 * rows2] - norm
    beta = norm_next / (norm + EPSILON)
    columns([size, beta])
    size_col = COEF[0:rows2, 0:1]
    beta_col = COEF[0:rows2, 1:2]

    v_in = [
        remote(V.at[1], V.at[2], v_send.at[0], v_recv.at[0], left),
        remote(V.at[1], V.at[0], v_send.at[1], v_recv.at[1], right),
    ]
    for copy in v_in:
        copy.wait_recv()
    for w in range(6):
        slot, cols = window(w)
        start = U[slot, :, cols]
        residual = start - size_col * V[slot, :, cols]
        direction = residual + beta_col * start
        split(direction, w)
        if slot == 1:
            W[:, cols] = direction
            W2[:, cols] = direction * oerr[:, pl.ds(pl.multiple_of(c * half + cols.start, block), block)]
    for p in range(10):
        s = PAIRS[p][0]
        cols = slice(s * block, (s + 1) * block)
        W2[:, cols] += product(p)

    w_copy = remote(W2.at[partner_rows, :], W3, w_send, w_recv, partner)
    w_copy.start()
    residual = U[1] - size_col * V[1]
    PP[0:rows2, :] = lane_sums(residual * residual)
    PP[rows2 : 2 * rows2, :] = lane_sums(W[...] * W2[...])
    sums, t_out = total(2 * rows2, R1B, R2B, (q1_send, q1_recv), (q2_send, q2_recv))
    size_next = sums[:, 0:rows2] / sums[:, rows2 : 2 * rows2]
    columns([size, beta, size_next])
    w_copy.wait_recv()
    size_here = COEF[core_rows, 0:1]
    beta_here = COEF[core_rows, 1:2]
    next_here = COEF[core_rows, 2:3]

    def finish(start, image, operated, where):
        residual = start - size_here * image
        direction = residual + beta_here * start
        x_out[:, where] = size_here * start + next_here * direction
        r_out[:, where] = residual - next_here * operated

    finish(innov[:, own_half], V[1, core_rows, :], W2[core_rows, :], own_half)
    finish(innov[:, other_half], V[2 - 2 * c, core_rows, :], W3[...], other_half)

    meta_back.wait_send()
    for copy in a_out + f_out + u_out + v_out + s_out + t_out + [w_copy]:
        copy.wait_send()


def body(anomalies, innovations, obs_error, positions, pair_far, block, nx):
    f32, bf16 = jnp.float32, jnp.bfloat16
    rows, width = anomalies.shape
    nobs, nmem = lax.axis_size("obs"), lax.axis_size("mem")
    nz = nobs // nx
    half, rows2, members, lanes = 2 * block, 2 * rows, rows * nmem, 128
    vmem = pl.BlockSpec(memory_space=pltpu.VMEM)
    dma = pltpu.SemaphoreType.DMA
    scratch = [
        pltpu.VMEM((3, members, half), bf16),
        pltpu.VMEM((half, members), bf16),
        pltpu.VMEM((3, rows2, half), f32),
        pltpu.VMEM((3, rows2, half), f32),
        pltpu.VMEM((6, 2 * rows2, block), bf16),
        pltpu.VMEM((10, block, block), bf16),
        pltpu.VMEM((10, block, block), bf16),
        pltpu.VMEM((10, block, block), f32),
        pltpu.VMEM((block, block), f32),
        pltpu.VMEM((2, half, lanes), f32),
        pltpu.VMEM((3, 8, half), f32),
        pltpu.VMEM((16, block), f32),
        pltpu.VMEM((4 * rows2, lanes), f32),
        pltpu.VMEM((rows2, half), f32),
        pltpu.VMEM((rows2, half), f32),
        pltpu.VMEM((rows, half), f32),
        pltpu.VMEM((lanes, lanes), f32),
        pltpu.VMEM((2 * nx, 4 * rows2), f32),
        pltpu.VMEM((nz, 4 * rows2), f32),
        pltpu.VMEM((2 * nx, 2 * rows2), f32),
        pltpu.VMEM((nz, 2 * rows2), f32),
        dma((nmem,)), dma((nmem,)),
        dma((2, nmem)), dma((2, nmem)),
        dma((4,)), dma((4,)),
        dma, dma,
        dma((2,)), dma((2,)),
        dma, dma,
        dma((2 * nx,)), dma((2 * nx,)), dma((nz,)), dma((nz,)),
        dma((2 * nx,)), dma((2 * nx,)), dma((nz,)), dma((nz,)),
    ]
    return pl.pallas_call(
        functools.partial(kernel, block, nobs, nmem, nx),
        out_shape=[jax.ShapeDtypeStruct((rows, width), f32)] * 2,
        in_specs=[vmem] * 4 + [pl.BlockSpec(memory_space=pltpu.SMEM)],
        out_specs=[vmem] * 2,
        scratch_shapes=scratch,
        compiler_params=pltpu.CompilerParams(
            collective_id=0, has_side_effects=True, vmem_limit_bytes=56 * 1024 * 1024
        ),
        name="filter_steps",
    )(anomalies, innovations, obs_error[None, :], positions, pair_far)


def solution(mesh, block=B, nx=NX):
    in_specs = (P("mem", "obs"), P("mem", "obs"), P("obs"), P(None, "obs"), P("obs"))
    out_specs = (P("mem", "obs"), P("mem", "obs"))
    return jax.shard_map(
        functools.partial(body, block=block, nx=nx),
        mesh=mesh,
        in_specs=in_specs,
        out_specs=out_specs,
        check_vma=False,
    )
```

time: 695 us -> 73 us (0.11)
  the two profiles are of different devices: /device:TPU:128 before, /device:TPU:1 now
where the time goes in v1:
time: 73 us; the launch traced here: 72.8 us
  Pallas kernels  69.8 us (96%)
  local copies, waits for them, and re-layouts  2.42 us (3%)
    pallas_call x1, Pallas kernels, body(): pl.pallas_call(functools.partial(kernel, block, nobs, nmem, nx), out_shap...  69.8 us
    unnamed x4, local copies, waits for them, and re-layouts  2.42 us

profile of v1, /device:TPU:1, one launch (start us, length us, event | category | flops | bytes accessed | tf_op | source)
XLA Modules:
  0.0 72.8 jit_solution(14015821045335891765)
XLA Ops:
  0.6 69.8 %filter_steps.1 = (f32[32,2048]{1,0:T(8,128)}, f32[32,2048]{1,0:T(8,128)}) custom-call(bf16[32,2048]{1,0:T(8,128)(2,1)} %anom.1, f32[32,2048]{1,0:T(8,128)} %innov.1, f32[1,2048]{1,0:T(1,128)} %bitcast.1, bf16[2,2048]{1,0:T(2,128)(2,1)} %places.1, s32[4]{0:T(128)} %far.1), custom_call_target="tpu_custom_call" | custom-call | tf_op jit(solution)/shard_map/filter_steps/pallas_call | solution.py:403
  70.4 0.0 copy-start
  70.4 1.7 %copy.9 = f32[32,2048]{1,0:T(8,128)} copy(f32[32,2048]{1,0:T(8,128)} %get-tuple-element.4) | data formatting | bytes 524288
  72.1 0.0 copy-done
  72.1 0.7 copy.10
Async XLA Ops:
  70.4 1.7 %copy-start = (f32[32,2048]{1,0:T(8,128)S(1)}, f32[32,2048]{1,0:T(8,128)}, u32[]{:S(2)}) copy-start(f32[32,2048]{1,0:T(8,128)} %get-tuple-element.5) | copy-start | bytes 786436

commit v2 on v1

v2 whole, which is shorter than its diff:
```python
import functools
import math

import jax
import jax.numpy as jnp
from jax import lax
from jax.experimental import pallas as pl
from jax.experimental.pallas import tpu as pltpu
from jax.sharding import PartitionSpec as P

B = 512
NX = 4
EPSILON = 1e-06
ROOT2 = math.sqrt(2.0)
SCALE = 48.0 * ROOT2
MESH = pl.DeviceIdType.MESH
LANES = 128
CHUNK = 32


def remote(src, dst, send, recv, device):
    return pltpu.make_async_remote_copy(
        src_ref=src, dst_ref=dst, send_sem=send, recv_sem=recv, device_id=device, device_id_type=MESH
    )


def kernel(
    block, nobs, nmem, nx,
    anom, innov, oerr, places, far, u1_out, u2_out, c_out,
    X, XT, U, V, UH, CH, CL, TP, PI, META, PP, W2, W3, SB, SR, G,
    a_send, a_recv, f_send, f_recv, u_send, u_recv, m_send, m_recv, v_send, v_recv, w_send, w_recv,
    e_send, e_recv, g_send, g_recv, reach, o_sem,
):
    f32, bf16 = jnp.float32, jnp.bfloat16
    half = 2 * block
    rows = anom.shape[0]
    rows2 = 2 * rows
    nz = nobs // nx
    o = lax.axis_index("obs")
    mm = lax.axis_index("mem")
    c = lax.rem(mm, 2)
    y2 = mm - c
    up = lax.rem(y2 + 2, nmem)
    down = lax.rem(y2 + nmem - 2, nmem)
    across_y = lax.rem(y2 + nmem // 2, nmem)
    pm = y2 + 1 - c
    z = lax.div(o, nx)
    x = lax.rem(o, nx)
    left = (lax.rem(o + nobs - 1 + c, nobs), pm)
    right = (lax.rem(o + c, nobs), pm)
    partner = (o, pm)
    far_to = (lax.rem(o + nobs + 1 - 2 * c, nobs), mm)
    far_from = (lax.rem(o + nobs - 1 + 2 * c, nobs), mm)
    off_chip = (lax.rem(o + nobs - 1 + 2 * c, nobs), pm)

    def peer(dz, dx):
        return (lax.rem(z + dz + nz, nz) * nx + lax.rem(x + dx + nx, nx), mm)

    barrier = pltpu.get_barrier_semaphore()
    near = [partner, left, right, far_to, far_from]
    near += [(o, y + k) for y in (up, down) for k in range(2)]
    near += [peer(0, dx) for dx in range(1, nx)]
    near += [peer(dz, 0) for dz in sorted({1, nz - 1})]
    for device in near:
        pl.semaphore_signal(barrier, inc=1, device_id=device, device_id_type=MESH)

    own_rows = pl.ds(pl.multiple_of(mm * rows, rows), rows)
    core_rows = pl.ds(pl.multiple_of(c * rows, rows), rows)
    partner_rows = pl.ds(pl.multiple_of((1 - c) * rows, rows), rows)
    own_half = pl.ds(pl.multiple_of(c * half, half), half)
    other_half = pl.ds(pl.multiple_of((1 - c) * half, half), half)
    pf = places[...].astype(f32) * ROOT2
    for h in range(2):
        flags = jnp.concatenate(
            [jnp.full((1, block), far[2 * h + b].astype(f32), f32) for b in range(2)], axis=1
        )
        META[1 - c + h] = jnp.concatenate(
            [pf[:, h * half : (h + 1) * half], flags, jnp.zeros((5, half), f32)], axis=0
        )
    X[1, own_rows, :] = anom[:, own_half]
    pl.semaphore_wait(barrier, len(near))

    steps = [step for step in (1, 2, 4, 8) if 2 * step <= nz]

    def tell(k):
        for dz in sorted({steps[k], nz - steps[k]}):
            pl.semaphore_signal(reach.at[k], inc=1, device_id=peer(dz, 0), device_id_type=MESH)

    def hear(k):
        pl.semaphore_wait(reach.at[k], len({steps[k], nz - steps[k]}))

    def widen(k):
        if k < len(steps):
            hear(k)
            if k + 1 < len(steps):
                tell(k + 1)

    meta_copy = remote(META.at[1], META.at[2 - 2 * c], m_send, m_recv, off_chip)
    meta_copy.start()
    meta_back = remote(META.at[1], META.at[2 * c], m_send, m_recv, off_chip)

    def half_of(core):
        return pl.ds(pl.multiple_of(core * half, half), half)

    def rows_of(member):
        return pl.ds(pl.multiple_of(member * rows, rows), rows)

    a_out = []
    for core in range(2):
        k = lax.rem(c + core, 2)
        a_out.append(
            remote(anom.at[:, half_of(k)], X.at[1, own_rows, :], a_send.at[1 + core], a_recv.at[1 + c], (o, up + k))
        )
        a_out.append(
            remote(anom.at[:, half_of(k)], X.at[1, own_rows, :], a_send.at[3 + core], a_recv.at[3 + c], (o, down + k))
        )
    a_out.append(remote(anom.at[:, other_half], X.at[1, own_rows, :], a_send.at[0], a_recv.at[0], partner))
    for copy in a_out:
        copy.start()

    u_out = [
        remote(innov.at[:, own_half], U.at[2, core_rows, :], u_send.at[0], u_recv.at[0], left),
        remote(innov.at[:, own_half], U.at[0, core_rows, :], u_send.at[1], u_recv.at[1], right),
        remote(innov.at[:, other_half], U.at[1, core_rows, :], u_send.at[2], u_recv.at[2], partner),
        remote(innov.at[:, other_half], U.at[2 * c, core_rows, :], u_send.at[3], u_recv.at[3], far_to),
    ]
    u_in = [
        remote(innov.at[:, own_half], U.at[2, partner_rows, :], u_send.at[0], u_recv.at[0], left),
        remote(innov.at[:, own_half], U.at[0, partner_rows, :], u_send.at[1], u_recv.at[1], right),
        remote(innov.at[:, other_half], U.at[1, partner_rows, :], u_send.at[2], u_recv.at[2], partner),
        remote(innov.at[:, other_half], U.at[2 * c, core_rows, :], u_send.at[3], u_recv.at[3], far_to),
    ]

    sources = [mm, pm, down, down + 1, up, up + 1, across_y, across_y + 1]
    f_out, relays = [], []

    def arrived(k):
        piece = rows_of(sources[k])
        remote(anom.at[:, own_half], X.at[1, piece, :], a_send.at[k - 1], a_recv.at[k - 1], partner).wait_recv()

    def forward(k):
        piece = rows_of(sources[k])
        if k > 0:
            arrived(k)
        if k == 2:
            relays.append(remote(X.at[1, piece, :], X.at[1, piece, :], a_send.at[5], a_recv.at[5], (o, up + c)))
            relays[-1].start()
        if k == 5:
            relays.append(remote(X.at[1, piece, :], X.at[1, piece, :], a_send.at[6], a_recv.at[6], (o, down + c)))
            relays[-1].start()
        one = remote(X.at[1, piece, :], X.at[2, piece, :], f_send.at[0, k], f_recv.at[0], left)
        two = remote(X.at[1, piece, :], X.at[0, piece, :], f_send.at[1, k], f_recv.at[1], right)
        one.start()
        two.start()
        f_out.extend([one, two])

    forward(0)
    for copy in u_out:
        copy.start()
    tell(0)
    for h in range(2):
        U[1 - c + h, core_rows, :] = innov[:, h * half : (h + 1) * half]

    def columns(slot):
        for k in range(half // LANES):
            for axis in range(2):
                line = META[slot, axis : axis + 1, k * LANES : (k + 1) * LANES]
                at = slot * half + k * LANES
                PI[axis, at : at + LANES, :] = jnp.broadcast_to(line, (LANES, LANES)).T

    def taper(s, w):
        offset = w - 2 - s
        cols = slice(s * block, (s + 1) * block)
        along = META[1, 0:1, cols] - offset * ROOT2
        across = META[1, 1:2, cols]
        close = abs(offset) < 2
        base = (w - s) * block
        times = block // LANES

        def step(k, carry):
            at = pl.multiple_of(k * CHUNK, CHUNK)
            theirs = pl.ds(w * block + at, CHUNK)
            g = jnp.concatenate([PI[0, theirs, :]] * times, axis=1) - along
            h = jnp.concatenate([PI[1, theirs, :]] * times, axis=1) - across
            square = g * g + h * h
            if close:
                square = jnp.maximum(square, 1e-30)
            inverse = lax.rsqrt(square)
            y = square * inverse
            rest = jnp.maximum(2.0 * ROOT2 - y, 0.0)
            rest = rest * rest
            value = (rest * rest) * ((y - inverse) + 2.0 * ROOT2)
            if close:
                inner = (-3.0 * y + 0.125 * SCALE) * y + 0.3125 * SCALE / ROOT2
                inner = (inner * y - (5.0 / 6.0) * SCALE) * square + SCALE
                value = jnp.maximum(value, inner)
            TP[s, pl.ds(base + at, CHUNK), :] = value
            return carry

        lax.fori_loop(0, block // CHUNK, step, 0, unroll=2)

    columns(1)
    taper(0, 2)
    forward(1)
    taper(0, 3)
    taper(1, 2)
    forward(2)
    taper(1, 3)
    forward(5)
    meta_back.wait_recv()
    columns(0)
    columns(2)
    taper(0, 1)
    forward(3)
    taper(1, 4)
    forward(4)
    widen(0)
    taper(0, 0)
    taper(0, 4)
    taper(1, 1)
    taper(1, 5)
    widen(1)

    first = jnp.where(2 * o + c > 0, 1.0, 0.0).astype(f32)
    last = jnp.where(2 * o + c < 2 * nobs - 1, 1.0, 0.0).astype(f32)

    def turn(slot):
        part = 2 * LANES
        for k in range(half // part):
            at = slot * half + k * part
            XT[at : at + part, :] = X[slot, :, k * part : (k + 1) * part].T

    def couple(s, w):
        offset = w - 2 - s
        cols = slice(s * block, (s + 1) * block)
        at = slice((w - s) * block, (w - s + 1) * block)
        value = jnp.dot(
            XT[w * block : (w + 1) * block, :], X[1, :, cols], preferred_element_type=f32
        ) * TP[s, at, :]
        if w < 2 or w > 3:
            line = jnp.full((1, block), 1.0, f32) * (first if w < 2 else last)
            if offset == 2:
                line = line * META[1, 2:3, cols]
            if offset == -2:
                line = line * META[0, 2:3, cols]
            value = value * line
        high = value.astype(bf16)
        CH[s, at, :] = high
        CL[s, at, :] = (value - high.astype(f32)).astype(bf16)

    def split(values, slot):
        cols = slice(slot * half, (slot + 1) * half)
        high = values.astype(bf16)
        UH[0:rows2, cols] = high
        UH[rows2 : 2 * rows2, cols] = (values - high.astype(f32)).astype(bf16)

    factor = 1.0 / (SCALE * (rows * nmem - 1))

    def product(s, begin, end):
        cols = slice(begin * block, end * block)
        at = slice((begin - s) * block, (end - s) * block)
        full = jnp.dot(UH[:, cols], CH[s, at, :], preferred_element_type=f32)
        low = jnp.dot(UH[0:rows2, cols], CL[s, at, :], preferred_element_type=f32)
        return (full[0:rows2] + full[rows2:] + low) * factor

    def noise(s):
        return oerr[:, pl.ds(pl.multiple_of(c * half + s * block, block), block)]

    for k in (6, 7):
        forward(k)
    turn(1)
    for s in range(2):
        for w in (2, 3):
            couple(s, w)
    widen(2)
    u_in[2].wait_recv()
    split(U[1], 1)
    for s in range(2):
        cols = slice(s * block, (s + 1) * block)
        V[1, :, cols] = U[1, :, cols] * noise(s) + product(s, 2, 4)
    for k in (0, 1, 3):
        u_in[k].wait_recv()
    split(U[0], 0)
    split(U[2], 2)
    for slot, way in ((0, 1), (2, 0)):
        remote(X.at[1], X.at[slot], f_send.at[0, 0], f_recv.at[way], partner).wait_recv()
        turn(slot)
    for s in range(2):
        for w in range(s, 2):
            couple(s, w)
        for w in range(4, s + 5):
            couple(s, w)

    v_out = []
    for s in range(2):
        cols = slice(s * block, (s + 1) * block)
        V[1, :, cols] += product(s, s, 2) + product(s, 4, s + 5)
        v_out.append(remote(V.at[1, :, cols], V.at[2, :, cols], v_send.at[0, s], v_recv.at[0, s], left))
        v_out.append(remote(V.at[1, :, cols], V.at[0, :, cols], v_send.at[1, s], v_recv.at[1, s], right))
        v_out[-2].start()
        v_out[-1].start()

    widen(3)
    u1_copy = [pltpu.make_async_copy(V.at[1, core_rows, :], u1_out.at[:, own_half], o_sem.at[0])]
    u1_copy[0].start()

    def lane_sums(d, value):
        total = value[:, 0:LANES]
        for k in range(1, half // LANES):
            total = total + value[:, k * LANES : (k + 1) * LANES]
        for h in range(2):
            PP[(4 * h + d) * rows : (4 * h + d + 1) * rows, :] = total[h * rows : (h + 1) * rows]

    split(V[1], 1)
    for s in range(2):
        cols = slice(s * block, (s + 1) * block)
        W2[:, cols] = V[1, :, cols] * noise(s) + product(s, 2, 4)
    lane_sums(0, U[1] * U[1])
    lane_sums(1, U[1] * V[1])
    lane_sums(2, V[1] * V[1])
    for way, slot in ((1, 0), (0, 2)):
        for s in range(2):
            cols = slice(s * block, (s + 1) * block)
            remote(V.at[1, :, cols], V.at[slot, :, cols], v_send.at[way, s], v_recv.at[way, s], partner).wait_recv()
        split(V[slot], slot)
    for s in range(2):
        cols = slice(s * block, (s + 1) * block)
        W2[:, cols] += product(s, s, 2) + product(s, 4, s + 5)

    lane_sums(3, V[1] * W2[...])
    row = jnp.sum(PP[...].T, axis=0, keepdims=True)
    SB[0:1, :] = row[:, 0 : 4 * rows]
    SB[1:2, :] = row[:, 4 * rows :]
    e_copy = remote(SB.at[pl.ds(1 - c, 1), :], SR, e_send, e_recv, partner)
    e_copy.start()
    w_copy = remote(W2.at[partner_rows, :], W3, w_send, w_recv, partner)
    w_copy.start()
    e_copy.wait_recv()
    G[pl.ds(o, 1), :] = SB[pl.ds(c, 1), :] + SR[...]
    mine = G.at[pl.ds(o, 1), :]
    offsets = [(dz, dx) for dz in range(nz) for dx in range(nx) if dz or dx]
    offsets.sort(key=lambda d: -(min(d[0], nz - d[0]) + min(d[1], nx - d[1])))
    for dz, dx in offsets:
        remote(mine, mine, g_send, g_recv, peer(dz, dx)).start()
    u1_copy.append(
        pltpu.make_async_copy(V.at[2 - 2 * c, core_rows, :], u1_out.at[:, other_half], o_sem.at[1])
    )
    u2_copy = [
        pltpu.make_async_copy(W2.at[core_rows, :], u2_out.at[:, own_half], o_sem.at[2]),
        pltpu.make_async_copy(W3, u2_out.at[:, other_half], o_sem.at[3]),
    ]
    u1_copy[1].start()
    u2_copy[0].start()
    w_copy.wait_recv()
    u2_copy[1].start()
    rest = G.at[0 : nobs - 1, :]
    remote(rest, rest, g_send, g_recv, partner).wait_recv()
    sums = jnp.sum(G[...], axis=0, keepdims=True)

    norm = sums[:, 0:rows]
    cross = sums[:, rows : 2 * rows]
    image = sums[:, 2 * rows : 3 * rows]
    size = norm / cross
    norm_next = size * size * image - norm
    more = 1.0 + norm_next / (norm + EPSILON)
    curve = (more * cross - 2.0 * size * image) * more + size * size * sums[:, 3 * rows :]
    size_next = norm_next / curve
    place = lax.broadcasted_iota(jnp.int32, (LANES, rows), 0)
    table = jnp.where(place == 0, size + size_next * more, size * size_next)
    table = jnp.concatenate([table, jnp.zeros((LANES, LANES - rows), f32)], axis=1)
    c_out[...] = table.T[0:rows, :]

    for copy in [meta_copy] + a_out + relays + f_out + u_out + v_out + [e_copy, w_copy]:
        copy.wait_send()
    remote(rest, rest, g_send, g_recv, partner).wait_send()
    for copy in u1_copy + u2_copy:
        copy.wait()


def body(anomalies, innovations, obs_error, positions, pair_far, block, nx):
    f32, bf16 = jnp.float32, jnp.bfloat16
    rows, width = anomalies.shape
    nobs, nmem = lax.axis_size("obs"), lax.axis_size("mem")
    half, rows2, members = 2 * block, 2 * rows, rows * nmem
    vmem = pl.BlockSpec(memory_space=pltpu.VMEM)
    whole = pl.BlockSpec(memory_space=pl.ANY)
    dma = pltpu.SemaphoreType.DMA
    scratch = [
        pltpu.VMEM((3, members, half), bf16),
        pltpu.VMEM((3 * half, members), bf16),
        pltpu.VMEM((3, rows2, half), f32),
        pltpu.VMEM((3, rows2, half), f32),
        pltpu.VMEM((2 * rows2, 3 * half), bf16),
        pltpu.VMEM((2, 5 * block, block), bf16),
        pltpu.VMEM((2, 5 * block, block), bf16),
        pltpu.VMEM((2, 5 * block, block), f32),
        pltpu.VMEM((2, 3 * half, LANES), f32),
        pltpu.VMEM((3, 8, half), f32),
        pltpu.VMEM((8 * rows, LANES), f32),
        pltpu.VMEM((rows2, half), f32),
        pltpu.VMEM((rows, half), f32),
        pltpu.VMEM((2, 4 * rows), f32),
        pltpu.VMEM((1, 4 * rows), f32),
        pltpu.VMEM((nobs, 4 * rows), f32),
        dma((7,)), dma((7,)),
        dma((2, 8)), dma((2,)),
        dma((4,)), dma((4,)),
        dma, dma,
        dma((2, 2)), dma((2, 2)),
        dma, dma,
        dma, dma,
        dma, dma,
        pltpu.SemaphoreType.REGULAR((4,)),
        dma((4,)),
    ]
    image, again, factors = pl.pallas_call(
        functools.partial(kernel, block, nobs, nmem, nx),
        out_shape=[jax.ShapeDtypeStruct((rows, width), f32)] * 2 + [jax.ShapeDtypeStruct((rows, LANES), f32)],
        in_specs=[vmem] * 4 + [pl.BlockSpec(memory_space=pltpu.SMEM)],
        out_specs=[whole, whole, vmem],
        scratch_shapes=scratch,
        compiler_params=pltpu.CompilerParams(
            collective_id=0, has_side_effects=True, vmem_limit_bytes=56 * 1024 * 1024
        ),
        name="filter_steps",
    )(anomalies, innovations, obs_error[None, :], positions, pair_far)
    linear, square = factors[:, 0:1], factors[:, 1:2]
    return (
        linear * innovations - square * image,
        innovations - linear * image + square * again,
    )


def solution(mesh, block=B, nx=NX):
    in_specs = (P("mem", "obs"), P("mem", "obs"), P("obs"), P(None, "obs"), P("obs"))
    out_specs = (P("mem", "obs"), P("mem", "obs"))
    return jax.shard_map(
        functools.partial(body, block=block, nx=nx),
        mesh=mesh,
        in_specs=in_specs,
        out_specs=out_specs,
        check_vma=False,
    )
```

time: 73 us -> 53.6 us (0.73)
  Pallas kernels: 69.8 us -> 49.7 us
  other arithmetic: 0 us -> 1.95 us
  local copies, waits for them, and re-layouts: 2.42 us -> 0.98 us
    pallas_call x1, Pallas kernels: 69.8 us -> 49.7 us  [body(): pl.pallas_call(functools.partial(kernel, block, nobs, nmem, nx), out_shap...]
    unnamed x4 -> x2, local copies, waits for them, and re-layouts: 2.42 us -> 0.01 us
    add x0 -> x1, other arithmetic: none -> 1.95 us  [body(): innovations - linear * image + square * again]
    slice x0 -> x1, local copies, waits for them, and re-layouts: none -> 0.97 us  [body(): linear, square = (factors[:, 0:1], factors[:, 1:2])]
where the time goes in v2:
time: 53.6 us; the launch traced here: 53.3 us
  Pallas kernels  49.7 us (93%)
  other arithmetic  1.95 us (4%)
  local copies, waits for them, and re-layouts  0.98 us (2%)
  between operations  0.65 us (1%)
    pallas_call x1, Pallas kernels, body(): pl.pallas_call(functools.partial(kernel, block, nobs, nmem, nx), out_shap...  49.7 us
    add x1, other arithmetic, body(): innovations - linear * image + square * again  1.95 us

profile of v2, /device:TPU:1, one launch (start us, length us, event | category | flops | bytes accessed | tf_op | source)
XLA Modules:
  0.0 53.3 jit_solution(8373839657577751105)
XLA Ops:
  0.6 0.0 copy-start
  0.6 49.7 %filter_steps.1 = (f32[32,2048]{1,0:T(8,128)}, f32[32,2048]{1,0:T(8,128)}, f32[32,128]{1,0:T(8,128)}) custom-call(bf16[32,2048]{1,0:T(8,128)(2,1)} %anom.1, f32[32,2048]{1,0:T(8,128)} %innov.1, f32[1,2048]{1,0:T(1,128)} %bitcast.1, bf16[2,2048]{1,0:T(2,128)(2,1)} %places.1, s32[4]{0:T(128)} %far.1), custom_call_target="tpu_custom_call" | custom-call | tf_op jit(solution)/shard_map/filter_steps/pallas_call | solution.py:416
  50.3 1.0 %slice_reduce_fusion.1 = (f32[32]{0:T(128)S(1)}, f32[32]{0:T(128)S(1)}) fusion(f32[32,128]{1,0:T(8,128)} %get-tuple-element.5), kind=kLoop, calls=%fused_computation.3 | loop fusion | bytes 512 | tf_op jit(solution)/shard_map/slice | solution.py:427
  51.3 0.0 copy-done
  51.3 2.0 %multiply_add_fusion = (f32[32,2048]{1,0:T(8,128)}, f32[32,2048]{1,0:T(8,128)}) fusion(f32[32,2048]{1,0:T(8,128)} %get-tuple-element.7, f32[32,2048]{1,0:T(8,128)S(1)} %copy-done, f32[32,2048]{1,0:T(8,128)} %get-tuple-element.6, f32[32]{0:T(128)S(1)} %get-tuple-element.9, f32[32]{0:T(128)S(1)} %get-tuple-element.8), kind=kLoop, calls=%fused_computation | loop fusion | flops 458752 | bytes 1310976 | tf_op jit(solution)/shard_map/add | solution.py:430
Async XLA Ops:
  0.6 50.7 %copy-start = (f32[32,2048]{1,0:T(8,128)S(1)}, f32[32,2048]{1,0:T(8,128)}, u32[]{:S(2)}) copy-start(f32[32,2048]{1,0:T(8,128)} %innov.1) | copy-start | bytes 786436

commit v3 on v2

--- a/solution.py
+++ b/solution.py
@@ -106,14 +106,13 @@
         return pl.ds(pl.multiple_of(member * rows, rows), rows)
 
     a_out = []
-    for core in range(2):
-        k = lax.rem(c + core, 2)
-        a_out.append(
-            remote(anom.at[:, half_of(k)], X.at[1, own_rows, :], a_send.at[1 + core], a_recv.at[1 + c], (o, up + k))
-        )
-        a_out.append(
-            remote(anom.at[:, half_of(k)], X.at[1, own_rows, :], a_send.at[3 + core], a_recv.at[3 + c], (o, down + k))
-        )
+    for way, slot in ((up + c * (down - up), 1 + 3 * c), (down + c * (up - down), 3 - c)):
+        for core in range(2):
+            k = lax.rem(c + core, 2)
+            copy = remote(
+                anom.at[:, half_of(k)], X.at[1, own_rows, :], a_send.at[len(a_out) + 1], a_recv.at[slot], (o, way + k)
+            )
+            a_out.append(copy)
     a_out.append(remote(anom.at[:, other_half], X.at[1, own_rows, :], a_send.at[0], a_recv.at[0], partner))
     for copy in a_out:
         copy.start()
@@ -161,25 +160,26 @@
     for h in range(2):
         U[1 - c + h, core_rows, :] = innov[:, h * half : (h + 1) * half]
 
+    off_side, on_side = c, 1 - c
+
+    def span(start, size):
+        return pl.ds(start if isinstance(start, int) else pl.multiple_of(start, size), size)
+
     def columns(slot):
         for k in range(half // LANES):
             for axis in range(2):
                 line = META[slot, axis : axis + 1, k * LANES : (k + 1) * LANES]
-                at = slot * half + k * LANES
-                PI[axis, at : at + LANES, :] = jnp.broadcast_to(line, (LANES, LANES)).T
-
-    def taper(s, w):
-        offset = w - 2 - s
-        cols = slice(s * block, (s + 1) * block)
-        along = META[1, 0:1, cols] - offset * ROOT2
+                PI[axis, span(slot * half + k * LANES, LANES), :] = jnp.broadcast_to(line, (LANES, LANES)).T
+
+    def taper(s, w, close):
+        cols = span(s * block, block)
+        shift = (w - 2 - s) * ROOT2 if isinstance(w, int) else (w - 2 - s).astype(f32) * ROOT2
+        along = META[1, 0:1, cols] - shift
         across = META[1, 1:2, cols]
-        close = abs(offset) < 2
-        base = (w - s) * block
         times = block // LANES
 
         def step(k, carry):
-            at = pl.multiple_of(k * CHUNK, CHUNK)
-            theirs = pl.ds(w * block + at, CHUNK)
+            theirs = span(w * block + k * CHUNK, CHUNK)
             g = jnp.concatenate([PI[0, theirs, :]] * times, axis=1) - along
             h = jnp.concatenate([PI[1, theirs, :]] * times, axis=1) - across
             square = g * g + h * h
@@ -194,113 +194,154 @@
                 inner = (-3.0 * y + 0.125 * SCALE) * y + 0.3125 * SCALE / ROOT2
                 inner = (inner * y - (5.0 / 6.0) * SCALE) * square + SCALE
                 value = jnp.maximum(value, inner)
-            TP[s, pl.ds(base + at, CHUNK), :] = value
+            TP[s, span((w - s) * block + k * CHUNK, CHUNK), :] = value
             return carry
 
         lax.fori_loop(0, block // CHUNK, step, 0, unroll=2)
 
+    def cross_pair(side):
+        return 1 - side, 1 + 3 * side
+
+    def next_pair(side):
+        return side, 1 + 3 * side
+
+    def outer_pair(side):
+        return side, 5 * side
+
     columns(1)
-    taper(0, 2)
+    taper(0, 2, True)
+    columns(2 * on_side)
+    taper(0, 3, True)
     forward(1)
-    taper(0, 3)
-    taper(1, 2)
+    taper(1, 3, True)
+    taper(*next_pair(on_side), True)
     forward(2)
-    taper(1, 3)
+    taper(*cross_pair(on_side), False)
     forward(5)
-    meta_back.wait_recv()
-    columns(0)
-    columns(2)
-    taper(0, 1)
+    taper(*outer_pair(on_side), False)
     forward(3)
-    taper(1, 4)
     forward(4)
     widen(0)
-    taper(0, 0)
-    taper(0, 4)
-    taper(1, 1)
-    taper(1, 5)
+    meta_back.wait_recv()
+    columns(2 * off_side)
+    taper(*cross_pair(off_side), False)
+    taper(*next_pair(off_side), True)
+    forward(6)
+    taper(*outer_pair(off_side), False)
+    forward(7)
     widen(1)
-
-    first = jnp.where(2 * o + c > 0, 1.0, 0.0).astype(f32)
-    last = jnp.where(2 * o + c < 2 * nobs - 1, 1.0, 0.0).astype(f32)
 
     def turn(slot):
         part = 2 * LANES
         for k in range(half // part):
-            at = slot * half + k * part
-            XT[at : at + part, :] = X[slot, :, k * part : (k + 1) * part].T
-
-    def couple(s, w):
-        offset = w - 2 - s
-        cols = slice(s * block, (s + 1) * block)
-        at = slice((w - s) * block, (w - s + 1) * block)
+            XT[span(slot * half + k * part, part), :] = X[slot, :, k * part : (k + 1) * part].T
+
+    def couple(s, w, factor=None):
+        at = span((w - s) * block, block)
         value = jnp.dot(
-            XT[w * block : (w + 1) * block, :], X[1, :, cols], preferred_element_type=f32
+            XT[span(w * block, block), :], X[1, :, span(s * block, block)], preferred_element_type=f32
         ) * TP[s, at, :]
-        if w < 2 or w > 3:
-            line = jnp.full((1, block), 1.0, f32) * (first if w < 2 else last)
-            if offset == 2:
-                line = line * META[1, 2:3, cols]
-            if offset == -2:
-                line = line * META[0, 2:3, cols]
-            value = value * line
+        if factor is not None:
+            value = value * factor
         high = value.astype(bf16)
         CH[s, at, :] = high
         CL[s, at, :] = (value - high.astype(f32)).astype(bf16)
 
+    def present(side):
+        chain = 2 * o + c
+        edge = jnp.where(side == 0, 0, 2 * nobs - 1)
+        return jnp.where(chain == edge, 0.0, 1.0).astype(f32)
+
+    def listed(s, side):
+        return META[side, 2:3, span(s * block, block)] * present(side)
+
     def split(values, slot):
-        cols = slice(slot * half, (slot + 1) * half)
+        cols = span(slot * half, half)
         high = values.astype(bf16)
         UH[0:rows2, cols] = high
         UH[rows2 : 2 * rows2, cols] = (values - high.astype(f32)).astype(bf16)
 
     factor = 1.0 / (SCALE * (rows * nmem - 1))
 
-    def product(s, begin, end):
-        cols = slice(begin * block, end * block)
-        at = slice((begin - s) * block, (end - s) * block)
+    def multiply(s, first_row, first_block, count):
+        cols = span(first_block * block, count * block) if isinstance(first_block, int) else pl.ds(
+            pl.multiple_of(first_block * block, block), count * block
+        )
+        at = pl.ds(pl.multiple_of(first_row * block, block), count * block)
         full = jnp.dot(UH[:, cols], CH[s, at, :], preferred_element_type=f32)
         low = jnp.dot(UH[0:rows2, cols], CL[s, at, :], preferred_element_type=f32)
         return (full[0:rows2] + full[rows2:] + low) * factor
 
+    def own_product(s):
+        if s == 0:
+            return multiply(0, 2, 2, 2)
+        cols = slice(2 * block, 3 * block)
+        at = slice(3 * block, 4 * block)
+        turned = (((1,), (1,)), ((), ()))
+        full = lax.dot_general(UH[:, cols], CH[0, at, :], turned, preferred_element_type=f32)
+        low = lax.dot_general(UH[0:rows2, cols], CL[0, at, :], turned, preferred_element_type=f32)
+        return multiply(1, 2, 3, 1) + (full[0:rows2] + full[rows2:] + low) * factor
+
+    def cross_product(side):
+        return multiply(1 - side, 4 * side, 1 + 3 * side, 1)
+
+    def side_product(side):
+        return multiply(side, 3 * side, 4 * side, 2)
+
     def noise(s):
         return oerr[:, pl.ds(pl.multiple_of(c * half + s * block, block), block)]
 
-    for k in (6, 7):
-        forward(k)
+    def wait_anomalies(side):
+        remote(X.at[1], X.at[2 * side], f_send.at[0, 0], f_recv.at[1 - side], partner).wait_recv()
+
+    def couple_cross(side):
+        s, w = cross_pair(side)
+        couple(s, w, listed(s, side))
+
+    def couple_side(side):
+        couple(*next_pair(side), present(side))
+        s, w = outer_pair(side)
+        couple(s, w, listed(s, side))
+
     turn(1)
-    for s in range(2):
-        for w in (2, 3):
-            couple(s, w)
-    widen(2)
+    for s, w in ((0, 2), (0, 3), (1, 3)):
+        couple(s, w)
     u_in[2].wait_recv()
     split(U[1], 1)
     for s in range(2):
         cols = slice(s * block, (s + 1) * block)
-        V[1, :, cols] = U[1, :, cols] * noise(s) + product(s, 2, 4)
-    for k in (0, 1, 3):
-        u_in[k].wait_recv()
-    split(U[0], 0)
-    split(U[2], 2)
-    for slot, way in ((0, 1), (2, 0)):
-        remote(X.at[1], X.at[slot], f_send.at[0, 0], f_recv.at[way], partner).wait_recv()
-        turn(slot)
-    for s in range(2):
-        for w in range(s, 2):
-            couple(s, w)
-        for w in range(4, s + 5):
-            couple(s, w)
+        V[1, :, cols] = U[1, :, cols] * noise(s) + own_product(s)
+    remote(innov.at[:, own_half], U.at[2 * on_side, partner_rows, :], u_send.at[0], u_recv.at[1 - on_side], partner).wait_recv()
+    split(U[2 * on_side], 2 * on_side)
+    wait_anomalies(on_side)
+    turn(2 * on_side)
+    couple_cross(on_side)
+    couple_side(on_side)
+    V[1, :, span((1 - on_side) * block, block)] += cross_product(on_side)
+    V[1, :, span(on_side * block, block)] += side_product(on_side)
+    widen(2)
+    remote(innov.at[:, own_half], U.at[2 * off_side, partner_rows, :], u_send.at[0], u_recv.at[1 - off_side], partner).wait_recv()
+    u_in[3].wait_recv()
+    split(U[2 * off_side], 2 * off_side)
+    wait_anomalies(off_side)
+    turn(2 * off_side)
 
     v_out = []
-    for s in range(2):
-        cols = slice(s * block, (s + 1) * block)
-        V[1, :, cols] += product(s, s, 2) + product(s, 4, s + 5)
-        v_out.append(remote(V.at[1, :, cols], V.at[2, :, cols], v_send.at[0, s], v_recv.at[0, s], left))
-        v_out.append(remote(V.at[1, :, cols], V.at[0, :, cols], v_send.at[1, s], v_recv.at[1, s], right))
+
+    def send_image(s, part):
+        cols = span(s * block, block)
+        v_out.append(remote(V.at[1, :, cols], V.at[2, :, cols], v_send.at[0, part], v_recv.at[0, part], left))
+        v_out.append(remote(V.at[1, :, cols], V.at[0, :, cols], v_send.at[1, part], v_recv.at[1, part], right))
         v_out[-2].start()
         v_out[-1].start()
 
-    widen(3)
+    couple_cross(off_side)
+    V[1, :, span((1 - off_side) * block, block)] += cross_product(off_side)
+    send_image(1 - off_side, 0)
+    couple_side(off_side)
+    V[1, :, span(off_side * block, block)] += side_product(off_side)
+    send_image(off_side, 1)
+
     u1_copy = [pltpu.make_async_copy(V.at[1, core_rows, :], u1_out.at[:, own_half], o_sem.at[0])]
     u1_copy[0].start()
 
@@ -311,21 +352,29 @@
         for h in range(2):
             PP[(4 * h + d) * rows : (4 * h + d + 1) * rows, :] = total[h * rows : (h + 1) * rows]
 
+    def wait_image(side):
+        for part in range(2):
+            s = c if part == 0 else 1 - c
+            cols = span(s * block, block)
+            remote(
+                V.at[1, :, cols], V.at[2 * side, :, cols], v_send.at[0, part], v_recv.at[1 - side, part], partner
+            ).wait_recv()
+        split(V[2 * side], 2 * side)
+
     split(V[1], 1)
     for s in range(2):
         cols = slice(s * block, (s + 1) * block)
-        W2[:, cols] = V[1, :, cols] * noise(s) + product(s, 2, 4)
+        W2[:, cols] = V[1, :, cols] * noise(s) + own_product(s)
     lane_sums(0, U[1] * U[1])
     lane_sums(1, U[1] * V[1])
     lane_sums(2, V[1] * V[1])
-    for way, slot in ((1, 0), (0, 2)):
-        for s in range(2):
-            cols = slice(s * block, (s + 1) * block)
-            remote(V.at[1, :, cols], V.at[slot, :, cols], v_send.at[way, s], v_recv.at[way, s], partner).wait_recv()
-        split(V[slot], slot)
-    for s in range(2):
-        cols = slice(s * block, (s + 1) * block)
-        W2[:, cols] += product(s, s, 2) + product(s, 4, s + 5)
+    wait_image(on_side)
+    W2[:, span((1 - on_side) * block, block)] += cross_product(on_side)
+    W2[:, span(on_side * block, block)] += side_product(on_side)
+    widen(3)
+    wait_image(off_side)
+    W2[:, span((1 - off_side) * block, block)] += cross_product(off_side)
+    W2[:, span(off_side * block, block)] += side_product(off_side)
 
     lane_sums(3, V[1] * W2[...])
     row = jnp.sum(PP[...].T, axis=0, keepdims=True)
@@ -375,6 +424,12 @@
     remote(rest, rest, g_send, g_recv, partner).wait_send()
     for copy in u1_copy + u2_copy:
         copy.wait()
+
+
+def combine(start, image, again, factors, x_out, r_out):
+    linear, square = factors[:, 0:1], factors[:, 1:2]
+    x_out[...] = linear * start[...] - square * image[...]
+    r_out[...] = start[...] - linear * image[...] + square * again[...]
 
 
 def body(anomalies, innovations, obs_error, positions, pair_far, block, nx):
@@ -424,10 +479,14 @@
         ),
         name="filter_steps",
     )(anomalies, innovations, obs_error[None, :], positions, pair_far)
-    linear, square = factors[:, 0:1], factors[:, 1:2]
-    return (
-        linear * innovations - square * image,
-        innovations - linear * image + square * again,
+    return tuple(
+        pl.pallas_call(
+            combine,
+            out_shape=[jax.ShapeDtypeStruct((rows, width), f32)] * 2,
+            in_specs=[vmem] * 4,
+            out_specs=[vmem] * 2,
+            name="combine",
+        )(innovations, image, again, factors)
     )
 
 

time: 53.6 us -> 48.7 us (0.909)
  other arithmetic: 1.95 us -> 0 us
  Pallas kernels: 49.7 us -> 47.9 us
  local copies, waits for them, and re-layouts: 0.98 us -> 0 us
    pallas_call x1, Pallas kernels: 49.7 us -> 45.8 us  [body(): pl.pallas_call(functools.partial(kernel, block, nobs, nmem, nx), out_shap...]
    pallas_call x0 -> x1, Pallas kernels: none -> 2.05 us  [body(): pl.pallas_call(combine, out_shape=[jax.ShapeDtypeStruct((rows, width), f3...]
    add x1 -> x0, other arithmetic: 1.95 us -> none  [body(): innovations - linear * image + square * again]
    slice x1 -> x0, local copies, waits for them, and re-layouts: 0.97 us -> none  [body(): linear, square = (factors[:, 0:1], factors[:, 1:2])]
where the time goes in v3:
time: 48.7 us; the launch traced here: 48.5 us
  Pallas kernels  47.9 us (98%)
  between operations  0.64 us (1%)
    pallas_call x1, Pallas kernels, body(): pl.pallas_call(functools.partial(kernel, block, nobs, nmem, nx), out_shap...  45.8 us
    pallas_call x1, Pallas kernels, body(): pl.pallas_call(combine, out_shape=[jax.ShapeDtypeStruct((rows, width), f3...  2.05 us

profile of v3, /device:TPU:1, one launch (start us, length us, event | category | flops | bytes accessed | tf_op | source)
XLA Modules:
  0.0 48.5 jit_solution(14878318211127777232)
XLA Ops:
  0.6 45.8 %filter_steps.1 = (f32[32,2048]{1,0:T(8,128)}, f32[32,2048]{1,0:T(8,128)}, f32[32,128]{1,0:T(8,128)}) custom-call(bf16[32,2048]{1,0:T(8,128)(2,1)} %anom.1, f32[32,2048]{1,0:T(8,128)} %start.1, f32[1,2048]{1,0:T(1,128)} %bitcast.1, bf16[2,2048]{1,0:T(2,128)(2,1)} %places.1, s32[4]{0:T(128)} %far.1), custom_call_target="tpu_custom_call" | custom-call | tf_op jit(solution)/shard_map/filter_steps/pallas_call | solution.py:471
  46.5 2.0 %combine.1 = (f32[32,2048]{1,0:T(8,128)}, f32[32,2048]{1,0:T(8,128)}) custom-call(f32[32,2048]{1,0:T(8,128)} %start.1, f32[32,2048]{1,0:T(8,128)} %get-tuple-element.5.image, f32[32,2048]{1,0:T(8,128)} %get-tuple-element.6.again, f32[32,128]{1,0:T(8,128)} %get-tuple-element.7.factors), custom_call_target="tpu_custom_call" | custom-call | tf_op jit(solution)/shard_map/combine/pallas_call | solution.py:483

commit v4 on v3

--- a/solution.py
+++ b/solution.py
@@ -26,10 +26,10 @@
 
 def kernel(
     block, nobs, nmem, nx,
-    anom, innov, oerr, places, far, u1_out, u2_out, c_out,
-    X, XT, U, V, UH, CH, CL, TP, PI, META, PP, W2, W3, SB, SR, G,
+    anom, innov, oerr, places, far, x_out, r_out,
+    X, XT, U, V, UH, CH, CL, TP, PI, META, PP, W2, W3, SB, G, XO, RO,
     a_send, a_recv, f_send, f_recv, u_send, u_recv, m_send, m_recv, v_send, v_recv, w_send, w_recv,
-    e_send, e_recv, g_send, g_recv, reach, o_sem,
+    g_send, g_recv, reach, o_sem,
 ):
     f32, bf16 = jnp.float32, jnp.bfloat16
     half = 2 * block
@@ -53,13 +53,14 @@
     far_from = (lax.rem(o + nobs - 1 + 2 * c, nobs), mm)
     off_chip = (lax.rem(o + nobs - 1 + 2 * c, nobs), pm)
 
-    def peer(dz, dx):
-        return (lax.rem(z + dz + nz, nz) * nx + lax.rem(x + dx + nx, nx), mm)
+    def peer(dz, dx, dc=0):
+        return (lax.rem(z + dz, nz) * nx + lax.rem(x + dx, nx), pm if dc else mm)
 
     barrier = pltpu.get_barrier_semaphore()
     near = [partner, left, right, far_to, far_from]
     near += [(o, y + k) for y in (up, down) for k in range(2)]
-    near += [peer(0, dx) for dx in range(1, nx)]
+    near += [(off_chip[0], y + 1 - c) for y in (up, down)]
+    near += [peer(0, dx, dc) for dx in range(1, nx) for dc in range(2)]
     near += [peer(dz, 0) for dz in sorted({1, nz - 1})]
     for device in near:
         pl.semaphore_signal(barrier, inc=1, device_id=device, device_id_type=MESH)
@@ -141,12 +142,24 @@
         piece = rows_of(sources[k])
         if k > 0:
             arrived(k)
-        if k == 2:
-            relays.append(remote(X.at[1, piece, :], X.at[1, piece, :], a_send.at[5], a_recv.at[5], (o, up + c)))
+        if k in (2, 5):
+            way = up if k == 2 else down
+            slot = 5 if k == 2 else 6
+            relays.append(remote(X.at[1, piece, :], X.at[1, piece, :], a_send.at[slot], a_recv.at[slot], (o, way + c)))
+            relays.append(
+                remote(
+                    X.at[1, piece, :], X.at[2 - 2 * c, piece, :], f_send.at[0, slot + 1], f_recv.at[c],
+                    (off_chip[0], way + 1 - c),
+                )
+            )
+            relays[-2].start()
             relays[-1].start()
-        if k == 5:
-            relays.append(remote(X.at[1, piece, :], X.at[1, piece, :], a_send.at[6], a_recv.at[6], (o, down + c)))
-            relays[-1].start()
+        if k > 5:
+            f_out.append(
+                remote(X.at[1, piece, :], X.at[2 * c, piece, :], f_send.at[1, k], f_recv.at[1 - c], partner)
+            )
+            f_out[-1].start()
+            return
         one = remote(X.at[1, piece, :], X.at[2, piece, :], f_send.at[0, k], f_recv.at[0], left)
         two = remote(X.at[1, piece, :], X.at[0, piece, :], f_send.at[1, k], f_recv.at[1], right)
         one.start()
@@ -342,15 +355,14 @@
     V[1, :, span(off_side * block, block)] += side_product(off_side)
     send_image(off_side, 1)
 
-    u1_copy = [pltpu.make_async_copy(V.at[1, core_rows, :], u1_out.at[:, own_half], o_sem.at[0])]
-    u1_copy[0].start()
-
     def lane_sums(d, value):
         total = value[:, 0:LANES]
         for k in range(1, half // LANES):
             total = total + value[:, k * LANES : (k + 1) * LANES]
+        if d == 3:
+            return jnp.sum(total.T, axis=0, keepdims=True)
         for h in range(2):
-            PP[(4 * h + d) * rows : (4 * h + d + 1) * rows, :] = total[h * rows : (h + 1) * rows]
+            PP[(3 * h + d) * rows : (3 * h + d + 1) * rows, :] = total[h * rows : (h + 1) * rows]
 
     def wait_image(side):
         for part in range(2):
@@ -368,6 +380,7 @@
     lane_sums(0, U[1] * U[1])
     lane_sums(1, U[1] * V[1])
     lane_sums(2, V[1] * V[1])
+    early = jnp.sum(PP[0 : 3 * rows2, :].T, axis=0, keepdims=True)
     wait_image(on_side)
     W2[:, span((1 - on_side) * block, block)] += cross_product(on_side)
     W2[:, span(on_side * block, block)] += side_product(on_side)
@@ -376,33 +389,22 @@
     W2[:, span((1 - off_side) * block, block)] += cross_product(off_side)
     W2[:, span(off_side * block, block)] += side_product(off_side)
 
-    lane_sums(3, V[1] * W2[...])
-    row = jnp.sum(PP[...].T, axis=0, keepdims=True)
-    SB[0:1, :] = row[:, 0 : 4 * rows]
-    SB[1:2, :] = row[:, 4 * rows :]
-    e_copy = remote(SB.at[pl.ds(1 - c, 1), :], SR, e_send, e_recv, partner)
-    e_copy.start()
+    late = lane_sums(3, V[1] * W2[...])
+    for h in range(2):
+        SB[h : h + 1, :] = jnp.concatenate(
+            [early[:, 3 * h * rows : 3 * (h + 1) * rows], late[:, h * rows : (h + 1) * rows]], axis=1
+        )
+    mine = pl.ds(2 * o + c, 1)
+    G[mine, :] = SB[pl.ds(c, 1), :]
+    offsets = [(dz, dx, dc) for dz in range(nz) for dx in range(nx) for dc in range(2) if dz or dx or dc]
+    offsets.sort(key=lambda d: -(min(d[0], nz - d[0]) + min(d[1], nx - d[1])))
+    for dz, dx, dc in offsets:
+        which = 1 - c if dc else c
+        remote(SB.at[pl.ds(which, 1), :], G.at[mine, :], g_send, g_recv, peer(dz, dx, dc)).start()
     w_copy = remote(W2.at[partner_rows, :], W3, w_send, w_recv, partner)
     w_copy.start()
-    e_copy.wait_recv()
-    G[pl.ds(o, 1), :] = SB[pl.ds(c, 1), :] + SR[...]
-    mine = G.at[pl.ds(o, 1), :]
-    offsets = [(dz, dx) for dz in range(nz) for dx in range(nx) if dz or dx]
-    offsets.sort(key=lambda d: -(min(d[0], nz - d[0]) + min(d[1], nx - d[1])))
-    for dz, dx in offsets:
-        remote(mine, mine, g_send, g_recv, peer(dz, dx)).start()
-    u1_copy.append(
-        pltpu.make_async_copy(V.at[2 - 2 * c, core_rows, :], u1_out.at[:, other_half], o_sem.at[1])
-    )
-    u2_copy = [
-        pltpu.make_async_copy(W2.at[core_rows, :], u2_out.at[:, own_half], o_sem.at[2]),
-        pltpu.make_async_copy(W3, u2_out.at[:, other_half], o_sem.at[3]),
-    ]
-    u1_copy[1].start()
-    u2_copy[0].start()
     w_copy.wait_recv()
-    u2_copy[1].start()
-    rest = G.at[0 : nobs - 1, :]
+    rest = G.at[0 : 2 * nobs - 1, :]
     remote(rest, rest, g_send, g_recv, partner).wait_recv()
     sums = jnp.sum(G[...], axis=0, keepdims=True)
 
@@ -417,19 +419,36 @@
     place = lax.broadcasted_iota(jnp.int32, (LANES, rows), 0)
     table = jnp.where(place == 0, size + size_next * more, size * size_next)
     table = jnp.concatenate([table, jnp.zeros((LANES, LANES - rows), f32)], axis=1)
-    c_out[...] = table.T[0:rows, :]
-
-    for copy in [meta_copy] + a_out + relays + f_out + u_out + v_out + [e_copy, w_copy]:
+    PP[0:LANES, :] = table.T
+    linear, square = PP[0:rows, 0:1], PP[0:rows, 1:2]
+    o_copy = []
+    for k, (where, image, again) in enumerate(
+        ((own_half, V[1, core_rows, :], W2[core_rows, :]), (other_half, V[2 - 2 * c, core_rows, :], W3[...]))
+    ):
+        start = innov[:, where]
+        XO[:, where] = linear * start - square * image
+        RO[:, where] = start - linear * image + square * again
+        for n, (result, out) in enumerate(((XO, x_out), (RO, r_out))):
+            o_copy.append(pltpu.make_async_copy(result.at[:, where], out.at[:, where], o_sem.at[2 * k + n]))
+            o_copy[-1].start()
+
+    for copy in [meta_copy] + a_out + relays + f_out + u_out + v_out + [w_copy]:
         copy.wait_send()
     remote(rest, rest, g_send, g_recv, partner).wait_send()
-    for copy in u1_copy + u2_copy:
+    for copy in o_copy:
         copy.wait()
 
 
-def combine(start, image, again, factors, x_out, r_out):
-    linear, square = factors[:, 0:1], factors[:, 1:2]
-    x_out[...] = linear * start[...] - square * image[...]
-    r_out[...] = start[...] - linear * image[...] + square * again[...]
+def hand_over(x_in, r_in, x_out, r_out, sems):
+    copies = []
+    part = x_in.shape[0] // 4
+    for n, (source, target) in enumerate(((x_in, x_out), (r_in, r_out))):
+        for k in range(4):
+            at = slice(k * part, (k + 1) * part)
+            copies.append(pltpu.make_async_copy(source.at[at, :], target.at[at, :], sems.at[4 * n + k]))
+            copies[-1].start()
+    for copy in copies:
+        copy.wait()
 
 
 def body(anomalies, innovations, obs_error, positions, pair_far, block, nx):
@@ -455,8 +474,9 @@
         pltpu.VMEM((rows2, half), f32),
         pltpu.VMEM((rows, half), f32),
         pltpu.VMEM((2, 4 * rows), f32),
-        pltpu.VMEM((1, 4 * rows), f32),
-        pltpu.VMEM((nobs, 4 * rows), f32),
+        pltpu.VMEM((2 * nobs, 4 * rows), f32),
+        pltpu.VMEM((rows, width), f32),
+        pltpu.VMEM((rows, width), f32),
         dma((7,)), dma((7,)),
         dma((2, 8)), dma((2,)),
         dma((4,)), dma((4,)),
@@ -464,15 +484,14 @@
         dma((2, 2)), dma((2, 2)),
         dma, dma,
         dma, dma,
-        dma, dma,
         pltpu.SemaphoreType.REGULAR((4,)),
         dma((4,)),
     ]
-    image, again, factors = pl.pallas_call(
+    results = pl.pallas_call(
         functools.partial(kernel, block, nobs, nmem, nx),
-        out_shape=[jax.ShapeDtypeStruct((rows, width), f32)] * 2 + [jax.ShapeDtypeStruct((rows, LANES), f32)],
+        out_shape=[jax.ShapeDtypeStruct((rows, width), f32)] * 2,
         in_specs=[vmem] * 4 + [pl.BlockSpec(memory_space=pltpu.SMEM)],
-        out_specs=[whole, whole, vmem],
+        out_specs=[whole] * 2,
         scratch_shapes=scratch,
         compiler_params=pltpu.CompilerParams(
             collective_id=0, has_side_effects=True, vmem_limit_bytes=56 * 1024 * 1024
@@ -481,12 +500,13 @@
     )(anomalies, innovations, obs_error[None, :], positions, pair_far)
     return tuple(
         pl.pallas_call(
-            combine,
+            hand_over,
             out_shape=[jax.ShapeDtypeStruct((rows, width), f32)] * 2,
-            in_specs=[vmem] * 4,
-            out_specs=[vmem] * 2,
-            name="combine",
-        )(innovations, image, again, factors)
+            in_specs=[whole] * 2,
+            out_specs=[whole] * 2,
+            scratch_shapes=[dma((8,))],
+            name="hand_over",
+        )(*results)
     )
 
 

time: 48.7 us -> 64.2 us (1.32)
  Pallas kernels: 47.9 us -> 63.4 us
    pallas_call x1, Pallas kernels: 2.05 us -> 17.1 us  [body(): pl.pallas_call(hand_over, out_shape=[jax.ShapeDtypeStruct((rows, width),...]
where the time goes in v4:
time: 64.2 us; the launch traced here: 64 us
  Pallas kernels  63.4 us (99%)
    pallas_call x1, Pallas kernels, body(): pl.pallas_call(functools.partial(kernel, block, nobs, nmem, nx), out_shap...  46.3 us
    pallas_call x1, Pallas kernels, body(): pl.pallas_call(hand_over, out_shape=[jax.ShapeDtypeStruct((rows, width),...  17.1 us

profile of v4, /device:TPU:1, one launch (start us, length us, event | category | flops | bytes accessed | tf_op | source)
XLA Modules:
  0.0 64.0 jit_solution(1505955861089256456)
XLA Ops:
  0.6 46.3 %filter_steps.1 = (f32[32,2048]{1,0:T(8,128)}, f32[32,2048]{1,0:T(8,128)}) custom-call(bf16[32,2048]{1,0:T(8,128)(2,1)} %anom.1, f32[32,2048]{1,0:T(8,128)} %innov.1, f32[1,2048]{1,0:T(1,128)} %bitcast.1, bf16[2,2048]{1,0:T(2,128)(2,1)} %places.1, s32[4]{0:T(128)} %far.1), custom_call_target="tpu_custom_call" | custom-call | tf_op jit(solution)/shard_map/filter_steps/pallas_call | solution.py:490
  47.0 17.1 %hand_over.1 = (f32[32,2048]{1,0:T(8,128)}, f32[32,2048]{1,0:T(8,128)}) custom-call(f32[32,2048]{1,0:T(8,128)} %get-tuple-element.4.x_in, f32[32,2048]{1,0:T(8,128)} %get-tuple-element.5.r_in), custom_call_target="tpu_custom_call" | custom-call | tf_op jit(solution)/shard_map/hand_over/pallas_call | solution.py:502

commit v5 on v4

--- a/solution.py
+++ b/solution.py
@@ -26,8 +26,8 @@
 
 def kernel(
     block, nobs, nmem, nx,
-    anom, innov, oerr, places, far, x_out, r_out,
-    X, XT, U, V, UH, CH, CL, TP, PI, META, PP, W2, W3, SB, G, XO, RO,
+    anom, innov, oerr, places, far, u1_out, u2_out, c_out,
+    X, XT, U, V, UH, CH, CL, TP, PI, META, PP, W2, W3, SB, G,
     a_send, a_recv, f_send, f_recv, u_send, u_recv, m_send, m_recv, v_send, v_recv, w_send, w_recv,
     g_send, g_recv, reach, o_sem,
 ):
@@ -176,7 +176,7 @@
     off_side, on_side = c, 1 - c
 
     def span(start, size):
-        return pl.ds(start if isinstance(start, int) else pl.multiple_of(start, size), size)
+        return pl.ds(start if isinstance(start, int) else pl.multiple_of(start, min(size, 2 * LANES)), size)
 
     def columns(slot):
         for k in range(half // LANES):
@@ -249,16 +249,17 @@
         for k in range(half // part):
             XT[span(slot * half + k * part, part), :] = X[slot, :, k * part : (k + 1) * part].T
 
-    def couple(s, w, factor=None):
+    def couple(s, w, factor=None, part=slice(0, block)):
         at = span((w - s) * block, block)
+        size = part.stop - part.start
         value = jnp.dot(
-            XT[span(w * block, block), :], X[1, :, span(s * block, block)], preferred_element_type=f32
-        ) * TP[s, at, :]
+            XT[span(w * block, block), :], X[1, :, span(s * block + part.start, size)], preferred_element_type=f32
+        ) * TP[s, at, part]
         if factor is not None:
-            value = value * factor
+            value = value * factor[:, part]
         high = value.astype(bf16)
-        CH[s, at, :] = high
-        CL[s, at, :] = (value - high.astype(f32)).astype(bf16)
+        CH[s, at, part] = high
+        CL[s, at, part] = (value - high.astype(f32)).astype(bf16)
 
     def present(side):
         chain = 2 * o + c
@@ -276,13 +277,13 @@
 
     factor = 1.0 / (SCALE * (rows * nmem - 1))
 
-    def multiply(s, first_row, first_block, count):
+    def multiply(s, first_row, first_block, count, part=slice(0, block)):
         cols = span(first_block * block, count * block) if isinstance(first_block, int) else pl.ds(
             pl.multiple_of(first_block * block, block), count * block
         )
         at = pl.ds(pl.multiple_of(first_row * block, block), count * block)
-        full = jnp.dot(UH[:, cols], CH[s, at, :], preferred_element_type=f32)
-        low = jnp.dot(UH[0:rows2, cols], CL[s, at, :], preferred_element_type=f32)
+        full = jnp.dot(UH[:, cols], CH[s, at, part], preferred_element_type=f32)
+        low = jnp.dot(UH[0:rows2, cols], CL[s, at, part], preferred_element_type=f32)
         return (full[0:rows2] + full[rows2:] + low) * factor
 
     def own_product(s):
@@ -295,11 +296,11 @@
         low = lax.dot_general(UH[0:rows2, cols], CL[0, at, :], turned, preferred_element_type=f32)
         return multiply(1, 2, 3, 1) + (full[0:rows2] + full[rows2:] + low) * factor
 
-    def cross_product(side):
-        return multiply(1 - side, 4 * side, 1 + 3 * side, 1)
-
-    def side_product(side):
-        return multiply(side, 3 * side, 4 * side, 2)
+    def cross_product(side, part=slice(0, block)):
+        return multiply(1 - side, 4 * side, 1 + 3 * side, 1, part)
+
+    def side_product(side, part=slice(0, block)):
+        return multiply(side, 3 * side, 4 * side, 2, part)
 
     def noise(s):
         return oerr[:, pl.ds(pl.multiple_of(c * half + s * block, block), block)]
@@ -307,14 +308,14 @@
     def wait_anomalies(side):
         remote(X.at[1], X.at[2 * side], f_send.at[0, 0], f_recv.at[1 - side], partner).wait_recv()
 
-    def couple_cross(side):
+    def couple_cross(side, part=slice(0, block)):
         s, w = cross_pair(side)
-        couple(s, w, listed(s, side))
-
-    def couple_side(side):
-        couple(*next_pair(side), present(side))
+        couple(s, w, listed(s, side), part)
+
+    def couple_side(side, part=slice(0, block)):
+        couple(*next_pair(side), jnp.full((1, block), 1.0, f32) * present(side), part)
         s, w = outer_pair(side)
-        couple(s, w, listed(s, side))
+        couple(s, w, listed(s, side), part)
 
     turn(1)
     for s, w in ((0, 2), (0, 3), (1, 3)):
@@ -341,19 +342,27 @@
 
     v_out = []
 
-    def send_image(s, part):
-        cols = span(s * block, block)
-        v_out.append(remote(V.at[1, :, cols], V.at[2, :, cols], v_send.at[0, part], v_recv.at[0, part], left))
-        v_out.append(remote(V.at[1, :, cols], V.at[0, :, cols], v_send.at[1, part], v_recv.at[1, part], right))
+    quarter = block // 2
+    halves = [slice(0, quarter), slice(quarter, block)]
+
+    def send_image(s, k):
+        cols = span(s * block + halves[k % 2].start, quarter)
+        v_out.append(remote(V.at[1, :, cols], V.at[2, :, cols], v_send.at[0, k], v_recv.at[0, k], left))
+        v_out.append(remote(V.at[1, :, cols], V.at[0, :, cols], v_send.at[1, k], v_recv.at[1, k], right))
         v_out[-2].start()
         v_out[-1].start()
 
-    couple_cross(off_side)
-    V[1, :, span((1 - off_side) * block, block)] += cross_product(off_side)
-    send_image(1 - off_side, 0)
-    couple_side(off_side)
-    V[1, :, span(off_side * block, block)] += side_product(off_side)
-    send_image(off_side, 1)
+    for k, part in enumerate(halves):
+        couple_cross(off_side, part)
+        V[1, :, span((1 - off_side) * block + part.start, quarter)] += cross_product(off_side, part)
+        send_image(1 - off_side, k)
+    for k, part in enumerate(halves):
+        couple_side(off_side, part)
+        V[1, :, span(off_side * block + part.start, quarter)] += side_product(off_side, part)
+        send_image(off_side, 2 + k)
+
+    o_copy = [pltpu.make_async_copy(V.at[1, core_rows, :], u1_out.at[:, own_half], o_sem.at[0])]
+    o_copy[0].start()
 
     def lane_sums(d, value):
         total = value[:, 0:LANES]
@@ -365,11 +374,11 @@
             PP[(3 * h + d) * rows : (3 * h + d + 1) * rows, :] = total[h * rows : (h + 1) * rows]
 
     def wait_image(side):
-        for part in range(2):
-            s = c if part == 0 else 1 - c
-            cols = span(s * block, block)
+        for k in range(4):
+            s = c if k < 2 else 1 - c
+            cols = span(s * block + halves[k % 2].start, quarter)
             remote(
-                V.at[1, :, cols], V.at[2 * side, :, cols], v_send.at[0, part], v_recv.at[1 - side, part], partner
+                V.at[1, :, cols], V.at[2 * side, :, cols], v_send.at[0, k], v_recv.at[1 - side, k], partner
             ).wait_recv()
         split(V[2 * side], 2 * side)
 
@@ -382,6 +391,8 @@
     lane_sums(2, V[1] * V[1])
     early = jnp.sum(PP[0 : 3 * rows2, :].T, axis=0, keepdims=True)
     wait_image(on_side)
+    o_copy.append(pltpu.make_async_copy(V.at[2 * on_side, core_rows, :], u1_out.at[:, other_half], o_sem.at[1]))
+    o_copy[1].start()
     W2[:, span((1 - on_side) * block, block)] += cross_product(on_side)
     W2[:, span(on_side * block, block)] += side_product(on_side)
     widen(3)
@@ -403,7 +414,11 @@
         remote(SB.at[pl.ds(which, 1), :], G.at[mine, :], g_send, g_recv, peer(dz, dx, dc)).start()
     w_copy = remote(W2.at[partner_rows, :], W3, w_send, w_recv, partner)
     w_copy.start()
+    o_copy.append(pltpu.make_async_copy(W2.at[core_rows, :], u2_out.at[:, own_half], o_sem.at[2]))
+    o_copy[2].start()
     w_copy.wait_recv()
+    o_copy.append(pltpu.make_async_copy(W3, u2_out.at[:, other_half], o_sem.at[3]))
+    o_copy[3].start()
     rest = G.at[0 : 2 * nobs - 1, :]
     remote(rest, rest, g_send, g_recv, partner).wait_recv()
     sums = jnp.sum(G[...], axis=0, keepdims=True)
@@ -419,18 +434,7 @@
     place = lax.broadcasted_iota(jnp.int32, (LANES, rows), 0)
     table = jnp.where(place == 0, size + size_next * more, size * size_next)
     table = jnp.concatenate([table, jnp.zeros((LANES, LANES - rows), f32)], axis=1)
-    PP[0:LANES, :] = table.T
-    linear, square = PP[0:rows, 0:1], PP[0:rows, 1:2]
-    o_copy = []
-    for k, (where, image, again) in enumerate(
-        ((own_half, V[1, core_rows, :], W2[core_rows, :]), (other_half, V[2 - 2 * c, core_rows, :], W3[...]))
-    ):
-        start = innov[:, where]
-        XO[:, where] = linear * start - square * image
-        RO[:, where] = start - linear * image + square * again
-        for n, (result, out) in enumerate(((XO, x_out), (RO, r_out))):
-            o_copy.append(pltpu.make_async_copy(result.at[:, where], out.at[:, where], o_sem.at[2 * k + n]))
-            o_copy[-1].start()
+    c_out[...] = table.T[0:rows, :]
 
     for copy in [meta_copy] + a_out + relays + f_out + u_out + v_out + [w_copy]:
         copy.wait_send()
@@ -439,16 +443,10 @@
         copy.wait()
 
 
-def hand_over(x_in, r_in, x_out, r_out, sems):
-    copies = []
-    part = x_in.shape[0] // 4
-    for n, (source, target) in enumerate(((x_in, x_out), (r_in, r_out))):
-        for k in range(4):
-            at = slice(k * part, (k + 1) * part)
-            copies.append(pltpu.make_async_copy(source.at[at, :], target.at[at, :], sems.at[4 * n + k]))
-            copies[-1].start()
-    for copy in copies:
-        copy.wait()
+def combine(start, image, again, factors, x_out, r_out):
+    linear, square = factors[:, 0:1], factors[:, 1:2]
+    x_out[...] = linear * start[...] - square * image[...]
+    r_out[...] = start[...] - linear * image[...] + square * again[...]
 
 
 def body(anomalies, innovations, obs_error, positions, pair_far, block, nx):
@@ -475,23 +473,21 @@
         pltpu.VMEM((rows, half), f32),
         pltpu.VMEM((2, 4 * rows), f32),
         pltpu.VMEM((2 * nobs, 4 * rows), f32),
-        pltpu.VMEM((rows, width), f32),
-        pltpu.VMEM((rows, width), f32),
         dma((7,)), dma((7,)),
         dma((2, 8)), dma((2,)),
         dma((4,)), dma((4,)),
         dma, dma,
-        dma((2, 2)), dma((2, 2)),
+        dma((2, 4)), dma((2, 4)),
         dma, dma,
         dma, dma,
         pltpu.SemaphoreType.REGULAR((4,)),
         dma((4,)),
     ]
-    results = pl.pallas_call(
+    image, again, factors = pl.pallas_call(
         functools.partial(kernel, block, nobs, nmem, nx),
-        out_shape=[jax.ShapeDtypeStruct((rows, width), f32)] * 2,
+        out_shape=[jax.ShapeDtypeStruct((rows, width), f32)] * 2 + [jax.ShapeDtypeStruct((rows, LANES), f32)],
         in_specs=[vmem] * 4 + [pl.BlockSpec(memory_space=pltpu.SMEM)],
-        out_specs=[whole] * 2,
+        out_specs=[whole, whole, vmem],
         scratch_shapes=scratch,
         compiler_params=pltpu.CompilerParams(
             collective_id=0, has_side_effects=True, vmem_limit_bytes=56 * 1024 * 1024
@@ -500,13 +496,12 @@
     )(anomalies, innovations, obs_error[None, :], positions, pair_far)
     return tuple(
         pl.pallas_call(
-            hand_over,
+            combine,
             out_shape=[jax.ShapeDtypeStruct((rows, width), f32)] * 2,
-            in_specs=[whole] * 2,
-            out_specs=[whole] * 2,
-            scratch_shapes=[dma((8,))],
-            name="hand_over",
-        )(*results)
+            in_specs=[vmem] * 4,
+            out_specs=[vmem] * 2,
+            name="combine",
+        )(innovations, image, again, factors)
     )
 
 

time: 64.2 us -> 49 us (0.76)
  Pallas kernels: 63.4 us -> 48.2 us
    pallas_call x1, Pallas kernels: 17.1 us -> 2.05 us  [body(): pl.pallas_call(combine, out_shape=[jax.ShapeDtypeStruct((rows, width), f3...]
where the time goes in v5:
time: 49 us; the launch traced here: 48.9 us
  Pallas kernels  48.2 us (98%)
  between operations  0.64 us (1%)
    pallas_call x1, Pallas kernels, body(): pl.pallas_call(functools.partial(kernel, block, nobs, nmem, nx), out_shap...  46.2 us
    pallas_call x1, Pallas kernels, body(): pl.pallas_call(combine, out_shape=[jax.ShapeDtypeStruct((rows, width), f3...  2.05 us

profile of v5, /device:TPU:1, one launch (start us, length us, event | category | flops | bytes accessed | tf_op | source)
XLA Modules:
  0.0 48.9 jit_solution(13298205753413758426)
XLA Ops:
  0.6 46.2 %filter_steps.1 = (f32[32,2048]{1,0:T(8,128)}, f32[32,2048]{1,0:T(8,128)}, f32[32,128]{1,0:T(8,128)}) custom-call(bf16[32,2048]{1,0:T(8,128)(2,1)} %anom.1, f32[32,2048]{1,0:T(8,128)} %start.1, f32[1,2048]{1,0:T(1,128)} %bitcast.1, bf16[2,2048]{1,0:T(2,128)(2,1)} %places.1, s32[4]{0:T(128)} %far.1), custom_call_target="tpu_custom_call" | custom-call | tf_op jit(solution)/shard_map/filter_steps/pallas_call | solution.py:486
  46.8 2.0 %combine.1 = (f32[32,2048]{1,0:T(8,128)}, f32[32,2048]{1,0:T(8,128)}) custom-call(f32[32,2048]{1,0:T(8,128)} %start.1, f32[32,2048]{1,0:T(8,128)} %get-tuple-element.5.image, f32[32,2048]{1,0:T(8,128)} %get-tuple-element.6.again, f32[32,128]{1,0:T(8,128)} %get-tuple-element.7.factors), custom_call_target="tpu_custom_call" | custom-call | tf_op jit(solution)/shard_map/combine/pallas_call | solution.py:498

commit v6 on v3

--- a/solution.py
+++ b/solution.py
@@ -78,88 +78,6 @@
             [pf[:, h * half : (h + 1) * half], flags, jnp.zeros((5, half), f32)], axis=0
         )
     X[1, own_rows, :] = anom[:, own_half]
-    pl.semaphore_wait(barrier, len(near))
-
-    steps = [step for step in (1, 2, 4, 8) if 2 * step <= nz]
-
-    def tell(k):
-        for dz in sorted({steps[k], nz - steps[k]}):
-            pl.semaphore_signal(reach.at[k], inc=1, device_id=peer(dz, 0), device_id_type=MESH)
-
-    def hear(k):
-        pl.semaphore_wait(reach.at[k], len({steps[k], nz - steps[k]}))
-
-    def widen(k):
-        if k < len(steps):
-            hear(k)
-            if k + 1 < len(steps):
-                tell(k + 1)
-
-    meta_copy = remote(META.at[1], META.at[2 - 2 * c], m_send, m_recv, off_chip)
-    meta_copy.start()
-    meta_back = remote(META.at[1], META.at[2 * c], m_send, m_recv, off_chip)
-
-    def half_of(core):
-        return pl.ds(pl.multiple_of(core * half, half), half)
-
-    def rows_of(member):
-        return pl.ds(pl.multiple_of(member * rows, rows), rows)
-
-    a_out = []
-    for way, slot in ((up + c * (down - up), 1 + 3 * c), (down + c * (up - down), 3 - c)):
-        for core in range(2):
-            k = lax.rem(c + core, 2)
-            copy = remote(
-                anom.at[:, half_of(k)], X.at[1, own_rows, :], a_send.at[len(a_out) + 1], a_recv.at[slot], (o, way + k)
-            )
-            a_out.append(copy)
-    a_out.append(remote(anom.at[:, other_half], X.at[1, own_rows, :], a_send.at[0], a_recv.at[0], partner))
-    for copy in a_out:
-        copy.start()
-
-    u_out = [
-        remote(innov.at[:, own_half], U.at[2, core_rows, :], u_send.at[0], u_recv.at[0], left),
-        remote(innov.at[:, own_half], U.at[0, core_rows, :], u_send.at[1], u_recv.at[1], right),
-        remote(innov.at[:, other_half], U.at[1, core_rows, :], u_send.at[2], u_recv.at[2], partner),
-        remote(innov.at[:, other_half], U.at[2 * c, core_rows, :], u_send.at[3], u_recv.at[3], far_to),
-    ]
-    u_in = [
-        remote(innov.at[:, own_half], U.at[2, partner_rows, :], u_send.at[0], u_recv.at[0], left),
-        remote(innov.at[:, own_half], U.at[0, partner_rows, :], u_send.at[1], u_recv.at[1], right),
-        remote(innov.at[:, other_half], U.at[1, partner_rows, :], u_send.at[2], u_recv.at[2], partner),
-        remote(innov.at[:, other_half], U.at[2 * c, core_rows, :], u_send.at[3], u_recv.at[3], far_to),
-    ]
-
-    sources = [mm, pm, down, down + 1, up, up + 1, across_y, across_y + 1]
-    f_out, relays = [], []
-
-    def arrived(k):
-        piece = rows_of(sources[k])
-        remote(anom.at[:, own_half], X.at[1, piece, :], a_send.at[k - 1], a_recv.at[k - 1], partner).wait_recv()
-
-    def forward(k):
-        piece = rows_of(sources[k])
-        if k > 0:
-            arrived(k)
-        if k == 2:
-            relays.append(remote(X.at[1, piece, :], X.at[1, piece, :], a_send.at[5], a_recv.at[5], (o, up + c)))
-            relays[-1].start()
-        if k == 5:
-            relays.append(remote(X.at[1, piece, :], X.at[1, piece, :], a_send.at[6], a_recv.at[6], (o, down + c)))
-            relays[-1].start()
-        one = remote(X.at[1, piece, :], X.at[2, piece, :], f_send.at[0, k], f_recv.at[0], left)
-        two = remote(X.at[1, piece, :], X.at[0, piece, :], f_send.at[1, k], f_recv.at[1], right)
-        one.start()
-        two.start()
-        f_out.extend([one, two])
-
-    forward(0)
-    for copy in u_out:
-        copy.start()
-    tell(0)
-    for h in range(2):
-        U[1 - c + h, core_rows, :] = innov[:, h * half : (h + 1) * half]
-
     off_side, on_side = c, 1 - c
 
     def span(start, size):
@@ -210,6 +128,88 @@
 
     columns(1)
     taper(0, 2, True)
+    pl.semaphore_wait(barrier, len(near))
+
+    steps = [step for step in (1, 2, 4, 8) if 2 * step <= nz]
+
+    def tell(k):
+        for dz in sorted({steps[k], nz - steps[k]}):
+            pl.semaphore_signal(reach.at[k], inc=1, device_id=peer(dz, 0), device_id_type=MESH)
+
+    def hear(k):
+        pl.semaphore_wait(reach.at[k], len({steps[k], nz - steps[k]}))
+
+    def widen(k):
+        if k < len(steps):
+            hear(k)
+            if k + 1 < len(steps):
+                tell(k + 1)
+
+    meta_copy = remote(META.at[1], META.at[2 - 2 * c], m_send, m_recv, off_chip)
+    meta_copy.start()
+    meta_back = remote(META.at[1], META.at[2 * c], m_send, m_recv, off_chip)
+
+    def half_of(core):
+        return pl.ds(pl.multiple_of(core * half, half), half)
+
+    def rows_of(member):
+        return pl.ds(pl.multiple_of(member * rows, rows), rows)
+
+    a_out = []
+    for way, slot in ((up + c * (down - up), 1 + 3 * c), (down + c * (up - down), 3 - c)):
+        for core in range(2):
+            k = lax.rem(c + core, 2)
+            copy = remote(
+                anom.at[:, half_of(k)], X.at[1, own_rows, :], a_send.at[len(a_out) + 1], a_recv.at[slot], (o, way + k)
+            )
+            a_out.append(copy)
+    a_out.append(remote(anom.at[:, other_half], X.at[1, own_rows, :], a_send.at[0], a_recv.at[0], partner))
+    for copy in a_out:
+        copy.start()
+
+    u_out = [
+        remote(innov.at[:, own_half], U.at[2, core_rows, :], u_send.at[0], u_recv.at[0], left),
+        remote(innov.at[:, own_half], U.at[0, core_rows, :], u_send.at[1], u_recv.at[1], right),
+        remote(innov.at[:, other_half], U.at[1, core_rows, :], u_send.at[2], u_recv.at[2], partner),
+        remote(innov.at[:, other_half], U.at[2 * c, core_rows, :], u_send.at[3], u_recv.at[3], far_to),
+    ]
+    u_in = [
+        remote(innov.at[:, own_half], U.at[2, partner_rows, :], u_send.at[0], u_recv.at[0], left),
+        remote(innov.at[:, own_half], U.at[0, partner_rows, :], u_send.at[1], u_recv.at[1], right),
+        remote(innov.at[:, other_half], U.at[1, partner_rows, :], u_send.at[2], u_recv.at[2], partner),
+        remote(innov.at[:, other_half], U.at[2 * c, core_rows, :], u_send.at[3], u_recv.at[3], far_to),
+    ]
+
+    sources = [mm, pm, down, down + 1, up, up + 1, across_y, across_y + 1]
+    f_out, relays = [], []
+
+    def arrived(k):
+        piece = rows_of(sources[k])
+        remote(anom.at[:, own_half], X.at[1, piece, :], a_send.at[k - 1], a_recv.at[k - 1], partner).wait_recv()
+
+    def forward(k):
+        piece = rows_of(sources[k])
+        if k > 0:
+            arrived(k)
+        if k == 2:
+            relays.append(remote(X.at[1, piece, :], X.at[1, piece, :], a_send.at[5], a_recv.at[5], (o, up + c)))
+            relays[-1].start()
+        if k == 5:
+            relays.append(remote(X.at[1, piece, :], X.at[1, piece, :], a_send.at[6], a_recv.at[6], (o, down + c)))
+            relays[-1].start()
+        one = remote(X.at[1, piece, :], X.at[2, piece, :], f_send.at[0, k], f_recv.at[0], left)
+        two = remote(X.at[1, piece, :], X.at[0, piece, :], f_send.at[1, k], f_recv.at[1], right)
+        one.start()
+        two.start()
+        f_out.extend([one, two])
+
+    forward(0)
+    for copy in u_out:
+        copy.start()
+    tell(0)
+    for h in range(2):
+        U[1 - c + h, core_rows, :] = innov[:, h * half : (h + 1) * half]
+
     columns(2 * on_side)
     taper(0, 3, True)
     forward(1)

time: 48.7 us -> 48.1 us (0.988)
  Pallas kernels: 47.9 us -> 47.3 us
    pallas_call x1, Pallas kernels: 45.8 us -> 45.2 us  [body(): pl.pallas_call(functools.partial(kernel, block, nobs, nmem, nx), out_shap...]
where the time goes in v6:
time: 48.1 us; the launch traced here: 47.9 us
  Pallas kernels  47.3 us (98%)
  between operations  0.64 us (1%)
    pallas_call x1, Pallas kernels, body(): pl.pallas_call(functools.partial(kernel, block, nobs, nmem, nx), out_shap...  45.2 us
    pallas_call x1, Pallas kernels, body(): pl.pallas_call(combine, out_shape=[jax.ShapeDtypeStruct((rows, width), f3...  2.05 us

profile of v6, /device:TPU:1, one launch (start us, length us, event | category | flops | bytes accessed | tf_op | source)
XLA Modules:
  0.0 47.9 jit_solution(1594983923576048880)
XLA Ops:
  0.6 45.2 %filter_steps.1 = (f32[32,2048]{1,0:T(8,128)}, f32[32,2048]{1,0:T(8,128)}, f32[32,128]{1,0:T(8,128)}) custom-call(bf16[32,2048]{1,0:T(8,128)(2,1)} %anom.1, f32[32,2048]{1,0:T(8,128)} %start.1, f32[1,2048]{1,0:T(1,128)} %bitcast.1, bf16[2,2048]{1,0:T(2,128)(2,1)} %places.1, s32[4]{0:T(128)} %far.1), custom_call_target="tpu_custom_call" | custom-call | tf_op jit(solution)/shard_map/filter_steps/pallas_call | solution.py:471
  45.8 2.0 %combine.1 = (f32[32,2048]{1,0:T(8,128)}, f32[32,2048]{1,0:T(8,128)}) custom-call(f32[32,2048]{1,0:T(8,128)} %start.1, f32[32,2048]{1,0:T(8,128)} %get-tuple-element.5.image, f32[32,2048]{1,0:T(8,128)} %get-tuple-element.6.again, f32[32,128]{1,0:T(8,128)} %get-tuple-element.7.factors), custom_call_target="tpu_custom_call" | custom-call | tf_op jit(solution)/shard_map/combine/pallas_call | solution.py:483

commit v7 on v6

--- a/solution.py
+++ b/solution.py
@@ -15,7 +15,7 @@
 SCALE = 48.0 * ROOT2
 MESH = pl.DeviceIdType.MESH
 LANES = 128
-CHUNK = 32
+CHUNK = 128
 
 
 def remote(src, dst, send, recv, device):
@@ -115,7 +115,7 @@
             TP[s, span((w - s) * block + k * CHUNK, CHUNK), :] = value
             return carry
 
-        lax.fori_loop(0, block // CHUNK, step, 0, unroll=2)
+        lax.fori_loop(0, block // CHUNK, step, 0)
 
     def cross_pair(side):
         return 1 - side, 1 + 3 * side

time: 48.1 us -> 48.1 us (level)
  no operation moved by 1% of the time
where the time goes in v7:
time: 48.1 us; the launch traced here: 47.9 us
  Pallas kernels  47.3 us (98%)
  between operations  0.64 us (1%)
    pallas_call x1, Pallas kernels, body(): pl.pallas_call(functools.partial(kernel, block, nobs, nmem, nx), out_shap...  45.2 us
    pallas_call x1, Pallas kernels, body(): pl.pallas_call(combine, out_shape=[jax.ShapeDtypeStruct((rows, width), f3...  2.05 us

profile of v7, /device:TPU:1, one launch (start us, length us, event | category | flops | bytes accessed | tf_op | source)
XLA Modules:
  0.0 47.9 jit_solution(11516802481862704370)
XLA Ops:
  0.6 45.2 %filter_steps.1 = (f32[32,2048]{1,0:T(8,128)}, f32[32,2048]{1,0:T(8,128)}, f32[32,128]{1,0:T(8,128)}) custom-call(bf16[32,2048]{1,0:T(8,128)(2,1)} %anom.1, f32[32,2048]{1,0:T(8,128)} %start.1, f32[1,2048]{1,0:T(1,128)} %bitcast.1, bf16[2,2048]{1,0:T(2,128)(2,1)} %places.1, s32[4]{0:T(128)} %far.1), custom_call_target="tpu_custom_call" | custom-call | tf_op jit(solution)/shard_map/filter_steps/pallas_call | solution.py:471
  45.8 2.0 %combine.1 = (f32[32,2048]{1,0:T(8,128)}, f32[32,2048]{1,0:T(8,128)}) custom-call(f32[32,2048]{1,0:T(8,128)} %start.1, f32[32,2048]{1,0:T(8,128)} %get-tuple-element.5.image, f32[32,2048]{1,0:T(8,128)} %get-tuple-element.6.again, f32[32,128]{1,0:T(8,128)} %get-tuple-element.7.factors), custom_call_target="tpu_custom_call" | custom-call | tf_op jit(solution)/shard_map/combine/pallas_call | solution.py:483
